TPU v7x, 256 devices: a whole 4x4x8 slice. The times are simulated.
256 devices in a mesh: tm: 32 (over x, y, core), space: 8 (over z).
Axes of the slice: x: 4, y: 4, z: 8, core: 2. Of those that a mesh axis runs over, the one named last changes fastest.
Arguments:
- frames_in: bfloat16 [256, 32, 64, 256], P('tm', 'space'), may hold values from -6 to 6
- cotangent: bfloat16 [256, 32, 64, 256], P('tm', 'space'), may hold values from -6 to 6
- spatial: bfloat16 [3, 3, 256, 256], replicated, may hold values from -0.125 to 0.125
- temporal: bfloat16 [3, 256, 256], replicated, may hold values from -0.375 to 0.375
- norm_gain: float32 [256], replicated, may hold values from 0.5 to 2
- norm_shift: float32 [256], replicated, may hold values from -3 to 3
- clip_frames: int32 [2], replicated, may hold values from 32 to 216, as said below
- dilation: int32 [2], replicated, may hold values from 1 to 8, as said below
Outputs:
- out_frames: bfloat16 [256, 32, 64, 256], P('tm', 'space')
- in_grad: bfloat16 [256, 32, 64, 256], P('tm', 'space')
- spatial_grad: float32 [3, 3, 256, 256], replicated
- temporal_grad: float32 [3, 256, 256], replicated
Inputs may be any that keep to these rules, and one draw needn't show every extreme that they name: `clip_frames`: the two clips are packed in order from slot 0 and fill at least 248 and at most 256 slots together; one of them has exactly 216 frames. One of the two clips has dilation 8.
All inputs are finite; a program needn't handle non-finite values.
Results may differ from a plain program's by a relative error of at most 0.0055.
Values may be sent and summed in bfloat16 or wider, within the bound.
A program may use at most 128 MiB of HBM per device.

v0:
```python
import jax
import jax.numpy as jnp
from jax import lax
from jax.sharding import PartitionSpec as P

GROUPS = 32
DMAX = 8


NORM_EPS = 1e-05


def extended(x, sides, width):
    for axis, dim in sides:
        size, length = (lax.axis_size(axis), x.shape[dim])
        up = [(i, (i + 1) % size) for i in range(size - 1)]
        down = [(j, i) for i, j in up]
        last = lax.slice_in_dim(x, length - width, length, axis=dim)
        initial = lax.slice_in_dim(x, 0, width, axis=dim)
        before = lax.ppermute(last, axis, up)
        after = lax.ppermute(initial, axis, down)
        x = jnp.concatenate([before, x, after], axis=dim)
    return x


def slot_tables(frame_ids, clip_frames):
    filled = clip_frames[0] + clip_frames[1]
    usable = (frame_ids >= 0) & (frame_ids < filled)
    clip_ids = (frame_ids >= clip_frames[0]).astype(jnp.int32)
    return (usable, clip_ids)


def shifted_pieces(source, first_frame, out_first, frame_count, clip_frames, dilation, direction):
    frame_ids = out_first + jnp.arange(frame_count, dtype=jnp.int32)
    usable, clip_ids = slot_tables(frame_ids, clip_frames)
    results = []
    for tap_index in range(3):
        combined = jnp.zeros((frame_count,) + source.shape[1:], source.dtype)
        for which_clip in range(2):
            offset_val = direction * (tap_index - 1) * dilation[which_clip]
            target_ok, target_clip = slot_tables(frame_ids + offset_val, clip_frames)
            keep_mask = usable & target_ok & (clip_ids == which_clip) & (target_clip == which_clip)
            start_row = out_first + offset_val - first_frame
            shifted = lax.dynamic_slice_in_dim(source, start_row, frame_count, 0)
            combined = jnp.where(keep_mask[:, None, None], shifted, combined)
        results.append(combined)
    return results


def time_forward(act_src, first_frame, out_first, frame_count, clip_frames, dilation, temporal):
    pieces = shifted_pieces(act_src, first_frame, out_first, frame_count, clip_frames, dilation, 1)
    summed = jnp.zeros(pieces[0].shape, jnp.float32)
    for tap_index in range(3):
        summed = summed + jnp.dot(
            pieces[tap_index], temporal[tap_index], preferred_element_type=jnp.float32
        )
    return summed.astype(jnp.bfloat16)


def time_backward(
    act_src, grad_src, first_frame, out_first, frame_count, clip_frames, dilation, temporal
):
    pieces_act = shifted_pieces(
        act_src, first_frame, out_first, frame_count, clip_frames, dilation, 1
    )
    pieces_grad = shifted_pieces(
        grad_src, first_frame, out_first, frame_count, clip_frames, dilation, -1
    )
    channels = grad_src.shape[-1]
    own_grad = lax.dynamic_slice_in_dim(grad_src, out_first - first_frame, frame_count, 0)
    flat_grad = own_grad.reshape(-1, channels)
    back_sum = jnp.zeros(pieces_grad[0].shape, jnp.float32)
    weight_terms = []
    for tap_index in range(3):
        back_sum = back_sum + lax.dot_general(
            pieces_grad[tap_index],
            temporal[tap_index],
            (((2,), (1,)), ((), ())),
            preferred_element_type=jnp.float32,
        )
        weight_terms.append(
            lax.dot_general(
                pieces_act[tap_index].reshape(-1, channels),
                flat_grad,
                (((0,), (0,)), ((), ())),
                preferred_element_type=jnp.float32,
            )
        )
    return (back_sum.astype(jnp.bfloat16), jnp.stack(weight_terms))


def widen(padded):
    return jnp.pad(padded, ((0, 0), (0, 0), (1, 1), (0, 0)))


def spatial_forward(padded, spatial):
    row_count = padded.shape[1] - 2
    col_count = padded.shape[2]
    wide = widen(padded)
    summed = jnp.zeros((padded.shape[0], row_count, col_count, spatial.shape[3]), jnp.float32)
    for offset_row in range(3):
        for offset_col in range(3):
            window = wide[
                :, offset_row : offset_row + row_count, offset_col : offset_col + col_count, :
            ]
            summed = summed + jnp.dot(
                window, spatial[offset_row, offset_col], preferred_element_type=jnp.float32
            )
    return summed


def spatial_backward(padded, spatial):
    row_count = padded.shape[1] - 2
    col_count = padded.shape[2]
    wide = widen(padded)
    summed = jnp.zeros((padded.shape[0], row_count, col_count, spatial.shape[2]), jnp.float32)
    for offset_row in range(3):
        for offset_col in range(3):
            window = wide[
                :,
                2 - offset_row : 2 - offset_row + row_count,
                2 - offset_col : 2 - offset_col + col_count,
                :,
            ]
            summed = summed + lax.dot_general(
                window,
                spatial[offset_row, offset_col],
                (((3,), (1,)), ((), ())),
                preferred_element_type=jnp.float32,
            )
    return summed


def weight_grad(padded, grad_conv):
    row_count = padded.shape[1] - 2
    col_count = padded.shape[2]
    channels = grad_conv.shape[-1]
    wide = widen(padded)
    flat_grad = grad_conv.reshape(-1, channels)
    outer_rows = []
    for offset_row in range(3):
        inner_cols = []
        for offset_col in range(3):
            window = wide[
                :, offset_row : offset_row + row_count, offset_col : offset_col + col_count, :
            ]
            inner_cols.append(
                lax.dot_general(
                    window.reshape(-1, window.shape[-1]),
                    flat_grad,
                    (((0,), (0,)), ((), ())),
                    preferred_element_type=jnp.float32,
                )
            )
        outer_rows.append(jnp.stack(inner_cols))
    return jnp.stack(outer_rows)


def group_fold(values):
    return values.reshape(values.shape[0], GROUPS, -1).sum(axis=2)


def spread_groups(values, group_size):
    return jnp.repeat(values, group_size, axis=-1)[:, None, None, :]


def normalize(conv_out, sum_first, sum_second, norm_gain, norm_shift, entries):
    group_size = conv_out.shape[-1] // GROUPS
    mean_val = sum_first / entries
    variance = sum_second / entries - mean_val * mean_val
    inv_std = lax.rsqrt(variance + NORM_EPS)
    inv_wide = spread_groups(inv_std, group_size)
    normed = (conv_out - spread_groups(mean_val, group_size)) * inv_wide
    shaped = normed * norm_gain + norm_shift
    return (normed, shaped, inv_wide)


def gradient_normed(grad_act, shaped, norm_gain):
    sigmoid_val = jax.nn.sigmoid(shaped)
    return (
        grad_act.astype(jnp.float32)
        * sigmoid_val
        * (1.0 + shaped * (1.0 - sigmoid_val))
        * norm_gain
    )


def norm_backward(grad_normed, normed, inv_wide, mean_first, mean_second):
    group_size = grad_normed.shape[-1] // GROUPS
    result = inv_wide * (
        grad_normed
        - spread_groups(mean_first, group_size)
        - normed * spread_groups(mean_second, group_size)
    )
    return result.astype(jnp.bfloat16)


def per_device(
    frames_in, cotangent, spatial, temporal, norm_gain, norm_shift, clip_frames, dilation
):
    slot_local, row_count, col_count, channels = frames_in.shape
    pixels = row_count * col_count
    entries = row_count * lax.axis_size("space") * col_count * (channels // GROUPS)
    tm_index = lax.axis_index("tm")
    padded = extended(frames_in, (("space", 1),), 1)
    conv_out = spatial_forward(padded, spatial)
    sum_first, sum_second = lax.psum(
        (
            group_fold(jnp.sum(conv_out, axis=(1, 2))),
            group_fold(jnp.sum(conv_out * conv_out, axis=(1, 2))),
        ),
        "space",
    )
    normed, shaped, inv_wide = normalize(
        conv_out, sum_first, sum_second, norm_gain, norm_shift, entries
    )
    frame_ids = tm_index * slot_local + jnp.arange(slot_local, dtype=jnp.int32)
    usable, clip_ids = slot_tables(frame_ids, clip_frames)
    activation = jnp.where(usable[:, None, None, None], jax.nn.silu(shaped), 0.0).astype(
        jnp.bfloat16
    )
    activation = activation.reshape(slot_local, pixels, channels)
    grad_rows = cotangent.reshape(slot_local, pixels, channels)
    pad_spec = ((DMAX, DMAX), (0, 0), (0, 0))
    act_tiles = lax.all_to_all(activation, "tm", split_axis=1, concat_axis=0, tiled=True)
    act_src = jnp.pad(act_tiles, pad_spec)
    frame_total = act_tiles.shape[0]
    out_tiles = time_forward(act_src, -DMAX, 0, frame_total, clip_frames, dilation, temporal)
    temporal_out = lax.all_to_all(out_tiles, "tm", split_axis=0, concat_axis=1, tiled=True)
    grad_tiles = lax.all_to_all(grad_rows, "tm", split_axis=1, concat_axis=0, tiled=True)
    back_tiles, temporal_part = time_backward(
        act_src,
        jnp.pad(grad_tiles, pad_spec),
        -DMAX,
        0,
        frame_total,
        clip_frames,
        dilation,
        temporal,
    )
    grad_act = lax.all_to_all(back_tiles, "tm", split_axis=0, concat_axis=1, tiled=True)
    out_frames = (
        frames_in.astype(jnp.float32) + temporal_out.reshape(frames_in.shape).astype(jnp.float32)
    ).astype(jnp.bfloat16)
    grad_normed = gradient_normed(grad_act.reshape(frames_in.shape), shaped, norm_gain)
    mean_first, mean_second = lax.psum(
        (
            group_fold(jnp.sum(grad_normed, axis=(1, 2))),
            group_fold(jnp.sum(grad_normed * normed, axis=(1, 2))),
        ),
        "space",
    )
    grad_conv = norm_backward(
        grad_normed, normed, inv_wide, mean_first / entries, mean_second / entries
    )
    conv_pad = extended(grad_conv, (("space", 1),), 1)
    in_grad = (cotangent.astype(jnp.float32) + spatial_backward(conv_pad, spatial)).astype(
        jnp.bfloat16
    )
    spatial_part = weight_grad(padded, grad_conv)
    spatial_grad, temporal_grad = lax.psum((spatial_part, temporal_part), ("tm", "space"))
    return (out_frames, in_grad, spatial_grad, temporal_grad)


def solution(mesh):
    placed = (
        P("tm", "space", None, None),
        P("tm", "space", None, None),
        P(),
        P(),
        P(),
        P(),
        P(),
        P(),
    )
    return jax.shard_map(
        per_device,
        mesh=mesh,
        in_specs=placed,
        out_specs=(P("tm", "space", None, None), P("tm", "space", None, None), P(), P()),
        check_vma=False,
    )
```

profile of v0, /device:TPU:1, one launch (start us, length us, event | category | flops | bytes accessed | tf_op | source)
XLA Modules:
  0.0 474.2 jit_solution(14364083972911447251)
XLA Ops:
  7.2 1.1 fusion.121
  8.2 4.4 collective-permute-start
  12.7 1.4 collective-permute-start.1
  14.1 2.8 copy.41
  16.9 8.1 %all-to-all-start.2 = ((bf16[8,256,256]{2,0,1:T(8,128)(2,1)}), bf16[8,256,256]{2,0,1:T(8,128)(2,1)}, u32[]{:S(2)}, u32[]{:S(2)}) async-start(bf16[8,256,256]{2,0,1:T(8,128)(2,1)} %bitcast.46), calls=%async_computation.2 | async-start | bytes 2097152 | tf_op jit(solution)/shard_map/all_to_all | solution.py:230
  32.1 2.0 compare_and_fusion
  34.8 2.7 fusion.70
  38.8 1.8 fusion.44
  40.5 1.8 fusion.47
  42.3 1.8 fusion.50
  44.1 1.8 fusion.53
  46.3 2.1 fusion.56
  48.3 1.7 fusion.62
  50.1 1.7 fusion.77
  51.8 1.5 copy.44
  53.4 2.8 select_select_fusion
  57.4 2.5 select_select_fusion.2
  61.1 1.6 copy.49
  62.6 7.4 %all-to-all-start.3 = ((bf16[256,8,256]{2,1,0:T(8,128)(2,1)}), bf16[256,8,256]{2,1,0:T(8,128)(2,1)S(1)}, u32[]{:S(2)}, u32[]{:S(2)}) async-start(bf16[256,8,256]{2,1,0:T(8,128)(2,1)} %copy.49), calls=%async_computation.3 | async-start | bytes 2097152 | tf_op jit(solution)/shard_map/all_to_all | solution.py:241
  70.0 8.3 %fusion.119 = (f32[8,256]{1,0:T(8,128)S(1)}, f32[8,256]{1,0:T(8,128)S(1)}, f32[8,4,64,256]{3,2,1,0:T(8,128)}) fusion(bf16[3,3,256,256]{3,2,1,0:T(8,128)(2,1)} %param.10, bf16[8,6,66,256]{3,2,1,0:T(8,128)(2,1)S(1)} %select_maximum_fusion.2, f32[8,4,64,256]{3,2,1,0:T(8,128)} %fusion.62, f32[8,4,64,256]{3,2,1,0:T(8,128)} %fusion.44, ...), kind=kOutput, calls=%fused_computation.182 | convolution fusion | flops 274198528 | bytes 20070400 | tf_op jit(solution)/shard_map/dot_general | solution.py:106
  78.8 17.5 %all-reduce.6 = (f32[8,32]{1,0:T(8,128)S(1)}, f32[8,32]{1,0:T(8,128)S(1)}) all-reduce(f32[8,32]{1,0:T(8,128)S(1)} %reduce_sum.75, f32[8,32]{1,0:T(8,128)S(1)} %reduce_sum.73), channel_id=1, replica_groups=mesh['tm'=32,'space'=8] {'space'}, use_global_device_ids=true, to_apply=%region_5.6 | all-reduce | flops 512 | bytes 4096 | tf_op jit(solution)/shard_map/psum | solution.py:207
  97.0 1.4 copy-done.3
  98.4 3.1 fusion.118
  101.9 11.9 %all-reduce.5 = (f32[8,32]{1,0:T(8,128)S(1)}, f32[8,32]{1,0:T(8,128)S(1)}) all-reduce(f32[8,32]{1,0:T(8,128)S(1)} %reduce_sum.79, f32[8,32]{1,0:T(8,128)S(1)} %reduce_sum.77), channel_id=1, replica_groups=mesh['tm'=32,'space'=8] {'space'}, use_global_device_ids=true, to_apply=%region_11.12 | all-reduce | flops 512 | bytes 4096 | tf_op jit(solution)/shard_map/psum | solution.py:246
  114.3 2.9 multiply_convert_fusion
  117.2 1.2 convolution_bitcast_fusion
  118.5 1.2 convolution_bitcast_fusion.1
  119.7 1.2 convolution_bitcast_fusion.6
  120.9 1.2 convolution_bitcast_fusion.7
  122.1 1.2 convolution_bitcast_fusion.8
  123.3 1.2 convolution_bitcast_fusion.9
  124.5 1.2 convolution_bitcast_fusion.10
  125.7 1.2 convolution_bitcast_fusion.11
  126.9 1.2 convolution_bitcast_fusion.5
  128.1 1.3 collective-permute-start.3
  129.4 4.7 collective-permute-start.2
  134.1 1.6 copy.31
  135.7 15.1 %all-to-all-start = ((bf16[8,256,256]{2,0,1:T(8,128)(2,1)}), bf16[8,256,256]{2,0,1:T(8,128)(2,1)}, u32[]{:S(2)}, u32[]{:S(2)}) async-start(bf16[8,256,256]{2,0,1:T(8,128)(2,1)} %copy.31), calls=%async_computation | async-start | bytes 2097152 | tf_op jit(solution)/shard_map/all_to_all | solution.py:225
  150.8 1.1 maximum_bitcast_fusion.1
  153.1 1.6 pad_maximum_fusion
  154.8 1.9 fusion.68
  156.7 1.9 select_maximum_fusion
  158.6 1.8 fusion.15
  160.4 1.8 fusion.17
  162.2 2.7 fusion.7
  164.9 1.8 fusion.19
  166.8 1.8 fusion.21
  168.6 1.8 fusion.23
  170.4 2.5 select_select_fusion.1
  172.9 3.3 convolution_bitcast_fusion.3
  177.3 1.5 copy.34
  178.8 2.5 select_select_fusion.4
  182.5 1.2 convolution_bitcast_fusion.4
  183.7 1.2 convolution_bitcast_fusion.2
  185.6 1.6 copy.39
  187.1 7.4 %all-to-all-start.1 = ((bf16[256,8,256]{2,1,0:T(8,128)(2,1)}), bf16[256,8,256]{2,1,0:T(8,128)(2,1)}, u32[]{:S(2)}, u32[]{:S(2)}) async-start(bf16[256,8,256]{2,1,0:T(8,128)(2,1)} %copy.39), calls=%async_computation.1 | async-start | bytes 2097152 | tf_op jit(solution)/shard_map/all_to_all | solution.py:229
  194.6 2.0 pad_maximum_fusion.1
  196.6 1.5 fusion.3
  198.5 7.0 %add_convert_fusion = bf16[8,4,64,256]{3,2,1,0:T(8,128)(2,1)} fusion(f32[8,4,64,256]{3,2,1,0:T(8,128)S(1)} %copy-done.8, f32[8,4,64,256]{3,2,1,0:T(8,128)} %fusion.15, f32[8,4,64,256]{3,2,1,0:T(8,128)} %fusion.17, f32[8,4,64,256]{3,2,1,0:T(8,128)} %fusion.68, f32[8,4,64,256]{3,2,1,0:T(8,128)} %fusion.19, f32[8,4,64,256]{3,2,1,0:T(8,128)} %fusion.21, ...), kind=kOutput, calls=%fused_computation.7 | convolution fusion | flops 274202624 | bytes 20054016 | tf_op jit(solution)/shard_map/dot_general | solution.py:125
  205.6 6.0 %all-to-all-done.1 = bf16[256,8,256]{2,1,0:T(8,128)(2,1)} async-done(((bf16[256,8,256]{2,1,0:T(8,128)(2,1)}), bf16[256,8,256]{2,1,0:T(8,128)(2,1)}, u32[]{:S(2)}, u32[]{:S(2)}) %all-to-all-start.1) | async-done | bytes 1048608 | tf_op jit(solution)/shard_map/all_to_all | solution.py:229
  211.5 1.5 convert_bitcast_fusion
  214.2 1.4 fusion.1
  215.6 247.6 %all-reduce.9.cloned.1.call-done = (f32[3,3,256,256]{3,2,1,0:T(8,128)}, f32[3,256,256]{2,1,0:T(8,128)}) async-done(((f32[3,3,256,256]{3,2,1,0:T(8,128)}, f32[3,256,256]{2,1,0:T(8,128)}), (f32[3,3,256,256]{3,2,1,0:T(8,128)}, f32[3,256,256]{2,1,0:T(8,128)})) %all-reduce.9.cloned.1.call-update) | async-done | bytes 3145744 | tf_op jit(solution)/shard_map/psum | solution.py:261
  463.2 3.3 copy.102
  (106 shorter events, 15.1 us)
Async XLA Ops:
  8.2 29.3 %collective-permute-start = (bf16[8,1,64,256]{3,2,1,0:T(8,128)(2,1)S(1)}, bf16[8,1,64,256]{3,2,1,0:T(8,128)(2,1)S(1)}, u32[]{:S(2)}, u32[]{:S(2)}) collective-permute-start(bf16[8,1,64,256]{3,2,1,0:T(8,128)(2,1)S(1)} %get-tuple-element.24), channel_id=1, source_target_pairs={{0,1},{1,2},{2,3},{3,4},{4,5},{5,6},{6,7},{8,9},{9,10},{10,11},{11... | collective-permute-start | bytes 786440 | tf_op jit(solution)/shard_map/ppermute | solution.py:20
  12.6 12.4 %copy-start.24 = (s32[2]{0:T(128)S(1)}, s32[2]{0:T(128)}, u32[]{:S(2)}) copy-start(s32[2]{0:T(128)} %param.15) | copy-start | bytes 28
  12.6 16.8 %copy-start.25 = (s32[2]{0:T(128)S(1)}, s32[2]{0:T(128)}, u32[]{:S(2)}) copy-start(s32[2]{0:T(128)} %param.14) | copy-start | bytes 28
  12.7 22.1 %copy-start = (bf16[8,4,64,256]{3,2,1,0:T(8,128)(2,1)S(1)}, bf16[8,4,64,256]{3,2,1,0:T(8,128)(2,1)}, u32[]{:S(2)}) copy-start(bf16[8,4,64,256]{3,2,1,0:T(8,128)(2,1)} %param.8) | copy-start | bytes 3145732
  12.7 24.8 %collective-permute-start.1 = (bf16[8,1,64,256]{3,2,1,0:T(8,128)(2,1)S(1)}, bf16[8,1,64,256]{3,2,1,0:T(8,128)(2,1)S(1)}, u32[]{:S(2)}, u32[]{:S(2)}) collective-permute-start(bf16[8,1,64,256]{3,2,1,0:T(8,128)(2,1)S(1)} %get-tuple-element.25), channel_id=1, source_target_pairs={{1,0},{2,1},{3,2},{4,3},{5,4},{6,5},{7,6},{9,8},{10,9},{11,10},{12... | collective-permute-start | bytes 786440 | tf_op jit(solution)/shard_map/ppermute | solution.py:21
  16.9 34.9 %all-to-all-start.2 = ((bf16[8,256,256]{2,0,1:T(8,128)(2,1)}), bf16[8,256,256]{2,0,1:T(8,128)(2,1)}, u32[]{:S(2)}, u32[]{:S(2)}) async-start(bf16[8,256,256]{2,0,1:T(8,128)(2,1)} %bitcast.46), calls=%async_computation.2 | async-start | bytes 2097152 | tf_op jit(solution)/shard_map/all_to_all | solution.py:230
  37.5 1.3 copy-start.11
  46.2 3.9 copy-start.9
  46.3 3.8 copy-start.6
  53.4 4.0 copy-start.4
  53.4 3.5 copy-start.15
  62.6 34.2 %all-to-all-start.3 = ((bf16[256,8,256]{2,1,0:T(8,128)(2,1)}), bf16[256,8,256]{2,1,0:T(8,128)(2,1)S(1)}, u32[]{:S(2)}, u32[]{:S(2)}) async-start(bf16[256,8,256]{2,1,0:T(8,128)(2,1)} %copy.49), calls=%async_computation.3 | async-start | bytes 2097152 | tf_op jit(solution)/shard_map/all_to_all | solution.py:241
  78.5 18.5 %copy-start.26 = (f32[256]{0:T(256)S(1)}, f32[256]{0:T(256)}, u32[]{:S(2)}) copy-start(f32[256]{0:T(256)} %param.13) | copy-start | bytes 3076
  78.5 18.5 %copy-start.27 = (f32[256]{0:T(256)S(1)}, f32[256]{0:T(256)}, u32[]{:S(2)}) copy-start(f32[256]{0:T(256)} %param.12) | copy-start | bytes 3076
  96.8 1.6 copy-start.3
  114.3 2.9 copy-start.7
  117.2 1.3 copy-start.10
  120.9 1.2 copy-start.1
  126.9 7.2 %copy-start.14 = (bf16[8,4,64,256]{3,2,1,0:T(8,128)(2,1)S(1)}, bf16[8,4,64,256]{3,2,1,0:T(8,128)(2,1)}, u32[]{:S(2)}) copy-start(bf16[8,4,64,256]{3,2,1,0:T(8,128)(2,1)} %get-tuple-element.15) | copy-start | bytes 3145732
  128.1 28.5 %collective-permute-start.3 = (bf16[8,1,64,256]{3,2,1,0:T(8,128)(2,1)S(1)}, bf16[8,1,64,256]{3,2,1,0:T(8,128)(2,1)S(1)}, u32[]{:S(2)}, u32[]{:S(2)}) collective-permute-start(bf16[8,1,64,256]{3,2,1,0:T(8,128)(2,1)S(1)} %get-tuple-element.16), channel_id=1, source_target_pairs={{1,0},{2,1},{3,2},{4,3},{5,4},{6,5},{7,6},{9,8},{10,9},{11,10},{12... | collective-permute-start | bytes 786440 | tf_op jit(solution)/shard_map/ppermute | solution.py:21
  129.4 27.2 %collective-permute-start.2 = (bf16[8,1,64,256]{3,2,1,0:T(8,128)(2,1)S(1)}, bf16[8,1,64,256]{3,2,1,0:T(8,128)(2,1)}, u32[]{:S(2)}, u32[]{:S(2)}) collective-permute-start(bf16[8,1,64,256]{3,2,1,0:T(8,128)(2,1)S(1)} %get-tuple-element.17), channel_id=1, source_target_pairs={{0,1},{1,2},{2,3},{3,4},{4,5},{5,6},{6,7},{8,9},{9,10},{10,11},{11... | collective-permute-start | bytes 786440 | tf_op jit(solution)/shard_map/ppermute | solution.py:20
  134.1 16.6 %copy-start.20 = (f32[1,256,256]{2,1,0:T(8,128)S(1)}, f32[1,256,256]{2,1,0:T(8,128)}, u32[]{:S(2)}) copy-start(f32[1,256,256]{2,1,0:T(8,128)} %convolution_bitcast_fusion.9) | copy-start | bytes 786436
  135.7 16.3 %copy-start.17 = (f32[1,256,256]{2,1,0:T(8,128)S(1)}, f32[1,256,256]{2,1,0:T(8,128)}, u32[]{:S(2)}) copy-start(f32[1,256,256]{2,1,0:T(8,128)} %convolution_bitcast_fusion) | copy-start | bytes 786436
  135.7 16.3 %copy-start.18 = (f32[1,256,256]{2,1,0:T(8,128)S(1)}, f32[1,256,256]{2,1,0:T(8,128)}, u32[]{:S(2)}) copy-start(f32[1,256,256]{2,1,0:T(8,128)} %convolution_bitcast_fusion.6) | copy-start | bytes 786436
  135.7 34.7 %all-to-all-start = ((bf16[8,256,256]{2,0,1:T(8,128)(2,1)}), bf16[8,256,256]{2,0,1:T(8,128)(2,1)}, u32[]{:S(2)}, u32[]{:S(2)}) async-start(bf16[8,256,256]{2,0,1:T(8,128)(2,1)} %copy.31), calls=%async_computation | async-start | bytes 2097152 | tf_op jit(solution)/shard_map/all_to_all | solution.py:225
  150.8 2.2 copy-start.16
  150.8 2.2 copy-start.19
  150.8 2.2 copy-start.23
  153.1 1.7 copy-start.12
  181.3 1.2 copy-start.5
  185.5 9.1 %copy-start.21 = (f32[1,256,256]{2,1,0:T(8,128)S(1)}, f32[1,256,256]{2,1,0:T(8,128)}, u32[]{:S(2)}) copy-start(f32[1,256,256]{2,1,0:T(8,128)} %convolution_bitcast_fusion.4) | copy-start | bytes 786436
  187.1 24.4 %all-to-all-start.1 = ((bf16[256,8,256]{2,1,0:T(8,128)(2,1)}), bf16[256,8,256]{2,1,0:T(8,128)(2,1)}, u32[]{:S(2)}, u32[]{:S(2)}) async-start(bf16[256,8,256]{2,1,0:T(8,128)(2,1)} %copy.39), calls=%async_computation.1 | async-start | bytes 2097152 | tf_op jit(solution)/shard_map/all_to_all | solution.py:229
  194.6 268.6 %all-reduce.9.cloned.1.call-start = ((), (), s32[]{:S(2)}) async-start(), calls=%async_computation.4 | async-start | bytes 6291456 | tf_op jit(solution)/shard_map/psum | solution.py:261
  196.6 1.7 copy-start.8
  196.6 1.9 copy-start.13
  213.0 1.2 copy-start.2
  463.2 3.3 copy-start.22
Sparse Core Ops, SparseCore 0:
  201.6 261.5 all-reduce.8
where the time goes:
time: 477 us; the launch traced here: 474 us
  waiting for transfers between devices  254 us (53%)
  matrix products  65.7 us (14%)
  starting transfers between devices  49.8 us (10%)
  other arithmetic  31.4 us (7%)
  blocking collectives  29.4 us (6%)
  local copies, waits for them, and re-layouts  24.2 us (5%)
  between operations  20 us (4%)
    psum x1, waiting for transfers between devices, per_device(): lax.psum((spatial_part, temporal_part), ('tm', 'space'))  248 us
    dot_general x9, matrix products, spatial_forward(): jnp.dot(window, spatial[offset_row, offset_col], preferred_element_type=j...  23.7 us
    dot_general x9, matrix products, spatial_backward(): lax.dot_general(window, spatial[offset_row, offset_col], (((3,), (1,)), (...  22.3 us
    psum x1, blocking collectives, per_device(): lax.psum((group_fold(jnp.sum(conv_out, axis=(1, 2))), group_fold(jnp.sum(...  17.5 us
    all_to_all x1, starting transfers between devices, per_device(): lax.all_to_all(activation, 'tm', split_axis=1, concat_axis=0, tiled=True)  15.1 us
    psum x1, blocking collectives, per_device(): lax.psum((group_fold(jnp.sum(grad_normed, axis=(1, 2))), group_fold(jnp.s...  11.9 us
    unnamed x60, local copies, waits for them, and re-layouts  11.2 us
    dot_general x9, matrix products, weight_grad(): lax.dot_general(window.reshape(-1, window.shape[-1]), flat_grad, (((0,),...  10.7 us
  transfers between devices with their start and end apart: 9, of which 2 were waited for; matrix products, arithmetic and copies ran while one was open for 14% of the time, Pallas kernels for 0%

commit v1 on v0

v1 whole, which is shorter than its diff:
```python
import functools

import jax
import jax.numpy as jnp
from jax import lax
from jax.experimental import pallas as pl
from jax.experimental.pallas import tpu as pltpu
from jax.sharding import PartitionSpec as P

MESH = pl.DeviceIdType.MESH
F32 = jnp.float32
BF16 = jnp.bfloat16
C = 256
FS = 8
ROWS = 4
COLS = 64
NX = 4
NY = 4
NTM = 32
NZ = 8
LINE = FS * COLS
ENTRIES = float(ROWS * NZ * COLS * 8)
EPS = 1e-05
MID = pl.ds(C, C)


def dot(a, b):
    return jnp.dot(a, b, preferred_element_type=F32)


def fold8(v):
    lane = lax.broadcasted_iota(jnp.int32, v.shape, 1)
    for step in (1, 2, 4):
        low = pltpu.roll(v, C - step, 1)
        high = pltpu.roll(v, step, 1)
        v = v + jnp.where((lane & step) == 0, low, high)
    return v


def shifted(v):
    n = v.shape[0]
    col = lax.broadcasted_iota(jnp.int32, v.shape, 0) & (COLS - 1)
    before = jnp.where(col == 0, 0.0, pltpu.roll(v, 1, 0))
    after = jnp.where(col == COLS - 1, 0.0, pltpu.roll(v, n - 1, 0))
    return before, after


def kernel(
    fr, ct, w_in, t_in, gain_ref, shift_ref, cf, dl,
    tout, ig_out, ag_out,
    xs3, xt, convf, dh, gn, a24, c24, pieces, at, gs3, w3, wt3, t3, tt3,
    st_loc, st_recv, st_fin, wg, s1h, r1, s1, s1c, r2, s2, s2c, r3, zf, zrecv, zag, agb, outv,
    lsem, bsend, brecv, ssend, srecv, rsend, rrecv,
):
    tm = lax.axis_index("tm")
    sp = lax.axis_index("space")
    core = lax.rem(tm, 2)
    yi = lax.rem(lax.div(tm, 2), NY)
    xi = lax.div(tm, 2 * NY)
    pair = tm + 1 - 2 * core
    tm_next = lax.rem(tm + 1, NTM)
    tm_prev = lax.rem(tm + NTM - 1, NTM)
    sp_next = lax.rem(sp + 1, NZ)
    sp_prev = lax.rem(sp + NZ - 1, NZ)

    def at_x(o):
        return (lax.rem(xi + o, NX) * NY + yi) * 2 + core

    def at_y(o):
        return (xi * NY + lax.rem(yi + o, NY)) * 2 + core

    def remote(src, dst, send, recv, device):
        copy = pltpu.make_async_remote_copy(
            src_ref=src, dst_ref=dst, send_sem=send, recv_sem=recv, device_id=device, device_id_type=MESH
        )
        copy.start()
        return copy

    loads = [
        pltpu.make_async_copy(fr.at[:, r], xs3.at[r + 1, :, :, MID], lsem.at[r]) for r in range(ROWS)
    ]
    loads.append(pltpu.make_async_copy(w_in, w3, lsem.at[4]))
    loads.append(pltpu.make_async_copy(t_in, t3, lsem.at[5]))
    loads.append(pltpu.make_async_copy(ct, c24.at[pl.ds(FS, FS)], lsem.at[6]))
    for load in loads:
        load.start()

    far = tm + (2 * core - 1)
    far = lax.rem(far + NTM, NTM)
    partners = [(pair, sp), (far, sp)]
    partners += [(tm, lax.rem(sp + o, NZ)) for o in range(1, NZ)]
    partners += [(at_x(o), sp) for o in range(1, NX)]
    partners += [(at_y(o), sp) for o in range(1, NY)]
    barrier = pltpu.get_barrier_semaphore()
    for partner in partners:
        pl.semaphore_signal(barrier, inc=1, device_id=partner, device_id_type=MESH)
    pl.semaphore_wait(barrier, len(partners))

    sends = []
    halo_x = [
        remote(fr.at[:, ROWS - 1], xs3.at[0, :, :, MID], bsend.at[0], brecv.at[0], (tm, sp_next)),
        remote(fr.at[:, 0], xs3.at[ROWS + 1, :, :, MID], bsend.at[1], brecv.at[1], (tm, sp_prev)),
    ]
    halo_c = [
        remote(ct, c24.at[pl.ds(0, FS)], bsend.at[2], brecv.at[2], (tm_next, sp)),
        remote(ct, c24.at[pl.ds(2 * FS, FS)], bsend.at[3], brecv.at[3], (tm_prev, sp)),
    ]
    sends += halo_x + halo_c

    def widen_row(ref, line, order, keep):
        v = ref[line, :, :, MID].reshape(LINE, C).astype(F32)
        if keep is not None:
            v = v * keep
            ref[line, :, :, MID] = v.astype(BF16).reshape(FS, COLS, C)
        before, after = shifted(v)
        if order < 0:
            before, after = after, before
        ref[line, :, :, pl.ds(0, C)] = before.astype(BF16).reshape(FS, COLS, C)
        ref[line, :, :, pl.ds(2 * C, C)] = after.astype(BF16).reshape(FS, COLS, C)

    def loop(lo, hi, body):
        def step(i, carry):
            body(i)
            return carry

        lax.fori_loop(lo, hi, step, 0)

    for r in range(ROWS):
        loads[r].wait()
    loop(1, ROWS + 1, lambda line: widen_row(xs3, line, 1, None))

    def conv_row(r):
        acc = dot(xs3[r].reshape(LINE, 3 * C), w3[0])
        acc = acc + dot(xs3[r + 1].reshape(LINE, 3 * C), w3[1])
        acc = acc + dot(xs3[r + 2].reshape(LINE, 3 * C), w3[2])
        acc = acc.reshape(FS, COLS, C)
        convf[r] = acc
        st_loc[0, pl.ds(0, FS)] += jnp.sum(acc, axis=1)
        st_loc[0, pl.ds(FS, FS)] += jnp.sum(acc * acc, axis=1)

    st_loc[0] = jnp.zeros((2 * FS, C), F32)
    loads[4].wait()
    loop(1, ROWS - 1, conv_row)

    def transpose_line(line):
        x = xs3[line, :, :, MID].reshape(LINE, C)
        xt[:, pl.ds(pl.multiple_of(line * LINE, LINE), LINE)] = x.T

    loop(1, ROWS + 1, transpose_line)

    def transpose_w(i):
        for j in range(3):
            wt3[i, pl.ds(j * C, C), :] = w3[i, pl.ds(j * C, C), :].T

    loop(0, 3, transpose_w)
    loads[5].wait()
    for k in range(3):
        tt3[pl.ds(k * C, C), :] = t3[pl.ds(k * C, C), :].T

    not_first = (sp > 0).astype(F32)
    not_last = (sp < NZ - 1).astype(F32)
    halo_x[0].wait_recv()
    widen_row(xs3, 0, 1, not_first)
    halo_x[1].wait_recv()
    widen_row(xs3, ROWS + 1, 1, not_last)
    loop(0, 2, lambda t: conv_row(t * (ROWS - 1)))

    def exchange_stats(phase):
        copies = []
        for o in range(1, NZ):
            n = phase * (NZ - 1) + o - 1
            copies.append(
                remote(
                    st_loc.at[phase], st_recv.at[phase, o - 1], ssend.at[n], srecv.at[n],
                    (tm, lax.rem(sp + o, NZ)),
                )
            )
        return copies

    def total_stats(phase, copies):
        total = st_loc[phase]
        for o in range(1, NZ):
            copies[o - 1].wait_recv()
            total = total + st_recv[phase, o - 1]
        return fold8(total) * (1.0 / ENTRIES)

    stats = exchange_stats(0)
    sends += stats
    loop(0, 2, lambda t: transpose_line(t * (ROWS + 1)))
    total = total_stats(0, stats)
    mean = total[0:FS]
    variance = total[FS : 2 * FS] - mean * mean
    st_fin[0] = mean
    st_fin[1] = lax.rsqrt(variance + EPS)

    first = cf[0]
    filled = cf[0] + cf[1]
    gain = gain_ref[...]
    bias = shift_ref[...]

    def activate(f):
        frame = tm * FS + f
        used = (frame < filled).astype(F32)
        v = convf[:, f].reshape(ROWS * COLS, C)
        normed = (v - st_fin[0, pl.ds(f, 1)]) * st_fin[1, pl.ds(f, 1)]
        shaped = normed * gain + bias
        sig = 0.5 * jnp.tanh(0.5 * shaped) + 0.5
        act = shaped * sig * used
        a24[FS + f] = act.astype(BF16).reshape(ROWS, COLS, C)
        convf[:, f] = normed.reshape(ROWS, COLS, C)
        dh[:, f] = (sig * (1.0 + shaped * (1.0 - sig)) * gain).reshape(ROWS, COLS, C)

    loop(0, FS, activate)
    own = pl.ds(FS, FS)
    halo_a = [
        remote(a24.at[own], a24.at[pl.ds(0, FS)], bsend.at[4], brecv.at[4], (tm_next, sp)),
        remote(a24.at[own], a24.at[pl.ds(2 * FS, FS)], bsend.at[5], brecv.at[5], (tm_prev, sp)),
    ]
    sends += halo_a

    def gather(source, f, direction):
        frame = tm * FS + f
        second = (frame >= first).astype(jnp.int32)
        gap = jnp.where(second == 1, dl[1], dl[0])
        for k in range(3):
            move = direction * (k - 1) * gap
            target = frame + move
            same = (target >= first).astype(jnp.int32) == second
            live = (frame < filled) & (target >= 0) & (target < filled) & same
            slot = jnp.clip(FS + f + move, 0, 3 * FS - 1)
            v = source[slot].astype(F32) * live.astype(F32)
            pieces[f, :, :, pl.ds(k * C, C)] = v.astype(BF16)

    loads[6].wait()
    for copy in halo_c:
        copy.wait_recv()

    def backward_time(f):
        gather(c24, f, -1)
        back = dot(pieces[f].reshape(ROWS * COLS, 3 * C), tt3[...]).astype(BF16).astype(F32)
        grad = back * dh[:, f].reshape(ROWS * COLS, C)
        gn[:, f] = grad.reshape(ROWS, COLS, C)
        normed = convf[:, f].reshape(ROWS * COLS, C)
        st_loc[1, pl.ds(f, 1)] = jnp.sum(grad, axis=0, keepdims=True)
        st_loc[1, pl.ds(FS + f, 1)] = jnp.sum(grad * normed, axis=0, keepdims=True)

    loop(0, FS, backward_time)
    stats = exchange_stats(1)
    sends += stats

    first_axis = [(at_y, yi), (at_x, xi), (at_y, yi), (at_x, xi)]
    second_axis = [(at_x, xi), (at_y, yi), (at_x, xi), (at_y, yi)]
    half = C // 2
    stage1 = [None] * 4
    stage2 = [None] * 4
    stage3 = [None] * 4

    def begin1(b):
        other = pl.ds(pl.multiple_of((1 - core) * half, half), half)
        s1h[b] = wg[b, other, :].astype(BF16)
        stage1[b] = remote(s1h.at[b], r1.at[b], rsend.at[b, 0], rrecv.at[b, 0], (pair, sp))
        sends.append(stage1[b])

    def begin2(b):
        stage1[b].wait_recv()
        mine = pl.ds(pl.multiple_of(core * half, half), half)
        v = wg[b, mine, :] + r1[b].astype(F32)
        s1[b] = v
        s1c[b] = v.astype(BF16)
        place, index = first_axis[b]
        stage2[b] = []
        for o in range(1, 4):
            rows = pl.ds(pl.multiple_of(lax.rem(index + o, 4) * 32, 32), 32)
            stage2[b].append(
                remote(
                    s1c.at[b, rows, :], r2.at[b, o - 1], rsend.at[b, o], rrecv.at[b, o], (place(o), sp)
                )
            )
        sends.extend(stage2[b])

    def begin3(b):
        index = first_axis[b][1]
        v = s1[b, pl.ds(pl.multiple_of(index * 32, 32), 32), :]
        for o in range(1, 4):
            stage2[b][o - 1].wait_recv()
            v = v + r2[b, o - 1].astype(F32)
        for q in range(4):
            part = v[(q // 2) * 16 : (q // 2) * 16 + 16, (q % 2) * 384 : (q % 2) * 384 + 384]
            s2[b, q] = part
            s2c[b, q] = part.astype(BF16)
        place, index = second_axis[b]
        stage3[b] = []
        for o in range(1, 4):
            stage3[b].append(
                remote(
                    s2c.at[b, lax.rem(index + o, 4)], r3.at[b, o - 1], rsend.at[b, 3 + o],
                    rrecv.at[b, 3 + o], (place(o), sp),
                )
            )
        sends.extend(stage3[b])

    def finish3(b):
        v = s2[b, second_axis[b][1]]
        for o in range(1, 4):
            stage3[b][o - 1].wait_recv()
            v = v + r3[b, o - 1].astype(F32)
        zf[pl.ds(2 * b, 2)] = v.reshape(2, 8, 384)

    def transpose_act(f):
        x = a24[FS + f].reshape(ROWS * COLS, C)
        at[:, pl.ds(pl.multiple_of(f * ROWS * COLS, ROWS * COLS), ROWS * COLS)] = x.T

    loop(0, FS, transpose_act)
    wg[0] = dot(at[...], pieces[...].reshape(FS * ROWS * COLS, 3 * C))
    begin1(0)

    total = total_stats(1, stats)
    st_fin[2] = total[0:FS]
    st_fin[3] = total[FS : 2 * FS]

    def conv_grad(r, f):
        v = st_fin[1, pl.ds(f, 1)] * (
            gn[r, f] - st_fin[2, pl.ds(f, 1)] - convf[r, f] * st_fin[3, pl.ds(f, 1)]
        )
        v16 = v.astype(BF16)
        before, after = shifted(v16.astype(F32))
        gs3[r + 1, f, :, pl.ds(0, C)] = after.astype(BF16)
        gs3[r + 1, f, :, MID] = v16
        gs3[r + 1, f, :, pl.ds(2 * C, C)] = before.astype(BF16)

    def conv_grad_edges(f):
        conv_grad(0, f)
        conv_grad(ROWS - 1, f)

    def conv_grad_inner(f):
        conv_grad(1, f)
        conv_grad(2, f)

    loop(0, FS, conv_grad_edges)
    halo_g = [
        remote(gs3.at[ROWS, :, :, MID], gs3.at[0, :, :, MID], bsend.at[6], brecv.at[6], (tm, sp_next)),
        remote(gs3.at[1, :, :, MID], gs3.at[ROWS + 1, :, :, MID], bsend.at[7], brecv.at[7], (tm, sp_prev)),
    ]
    sends += halo_g
    loop(0, FS, conv_grad_inner)
    begin2(0)

    for i in range(3):
        wg[i + 1] = dot(
            xt[:, pl.ds(i * LINE, ROWS * LINE)], gs3[pl.ds(1, ROWS)].reshape(ROWS * LINE, 3 * C)
        )
        begin1(i + 1)
    begin3(0)
    for b in (1, 2, 3):
        begin2(b)

    def in_row(r):
        acc = dot(gs3[r + 2].reshape(LINE, 3 * C), wt3[0])
        acc = acc + dot(gs3[r + 1].reshape(LINE, 3 * C), wt3[1])
        acc = acc + dot(gs3[r].reshape(LINE, 3 * C), wt3[2])
        acc = acc.reshape(FS, COLS, C) + c24[pl.ds(FS, FS), r].astype(F32)
        outv[0, :, r] = acc.astype(BF16)

    loop(1, ROWS - 1, in_row)
    for b in (1, 2, 3):
        begin3(b)
    halo_g[0].wait_recv()
    widen_row(gs3, 0, -1, not_first)
    halo_g[1].wait_recv()
    widen_row(gs3, ROWS + 1, -1, not_last)
    for b in range(4):
        finish3(b)
    z1 = []
    for o in range(1, NZ):
        q = lax.rem(sp + o, NZ)
        z1.append(remote(zf.at[q], zrecv.at[o - 1], ssend.at[13 + o], srecv.at[13 + o], (tm, q)))
    sends += z1
    loop(0, 2, lambda t: in_row(t * (ROWS - 1)))
    out_ig = pltpu.make_async_copy(outv.at[0], ig_out, lsem.at[7])
    out_ig.start()

    v = zf[sp]
    for o in range(1, NZ):
        z1[o - 1].wait_recv()
        v = v + zrecv[o - 1]
    zag[sp] = v
    z2 = []
    for o in range(1, NZ):
        q = lax.rem(sp + o, NZ)
        z2.append(remote(zag.at[sp], zag.at[sp], ssend.at[20 + o], srecv.at[20 + o], (tm, q)))
    sends += z2

    for copy in halo_a:
        copy.wait_recv()

    def forward_time(f):
        gather(a24, f, 1)
        outv[1, f] = (
            dot(pieces[f].reshape(ROWS * COLS, 3 * C), t3[...]).astype(BF16).reshape(ROWS, COLS, C)
        )

    loop(0, FS, forward_time)
    out_t = pltpu.make_async_copy(outv.at[1], tout, lsem.at[8])
    out_t.start()

    for copy in z2:
        copy.wait_recv()
    g3 = []
    for b in range(4):
        n1, n2 = first_axis[b][1], second_axis[b][1]
        agb[b, core, n1, n2] = zag[pl.ds(2 * b, 2)].reshape(16, 384).astype(BF16)
        place = second_axis[b][0]
        here = agb.at[b, core, n1, n2]
        g3.append(
            [remote(here, here, rsend.at[b, 6 + o], rrecv.at[b, 6 + o], (place(o), sp)) for o in range(1, 4)]
        )
        sends += g3[b]
    g2 = []
    for b in range(4):
        for copy in g3[b]:
            copy.wait_recv()
        place, n1 = first_axis[b]
        here = agb.at[b, core, n1]
        g2.append(
            [remote(here, here, rsend.at[b, 9 + o], rrecv.at[b, 9 + o], (place(o), sp)) for o in range(1, 4)]
        )
        sends += g2[b]
    g1 = []
    for b in range(4):
        for copy in g2[b]:
            copy.wait_recv()
        here = agb.at[b, core]
        g1.append(remote(here, here, rsend.at[b, 13], rrecv.at[b, 13], (pair, sp)))
    sends += g1
    out_g = []
    for b in range(4):
        g1[b].wait_recv()
        out_g.append(pltpu.make_async_copy(agb.at[b], ag_out.at[b], lsem.at[9 + b]))
        out_g[b].start()
    for copy in sends:
        copy.wait_send()
    out_ig.wait()
    out_t.wait()
    for copy in out_g:
        copy.wait()


def section(frames_in, cotangent, spatial, temporal, norm_gain, norm_shift, clip_frames, dilation):
    any_spec = pl.BlockSpec(memory_space=pl.ANY)
    vmem_spec = pl.BlockSpec(memory_space=pltpu.VMEM)
    smem_spec = pl.BlockSpec(memory_space=pltpu.SMEM)
    shape = (FS, ROWS, COLS, C)
    V = pltpu.VMEM
    DMA = pltpu.SemaphoreType.DMA
    tout, ig, ag = pl.pallas_call(
        kernel,
        out_shape=(
            jax.ShapeDtypeStruct(shape, BF16),
            jax.ShapeDtypeStruct(shape, BF16),
            jax.ShapeDtypeStruct((4, 2, 4, 4, 16, 384), BF16),
        ),
        in_specs=[any_spec] * 4 + [vmem_spec] * 2 + [smem_spec] * 2,
        out_specs=(any_spec, any_spec, any_spec),
        scratch_shapes=[
            V((ROWS + 2, FS, COLS, 3 * C), BF16),
            V((C, (ROWS + 2) * LINE), BF16),
            V((ROWS, FS, COLS, C), F32),
            V((ROWS, FS, COLS, C), F32),
            V((ROWS, FS, COLS, C), F32),
            V((3 * FS, ROWS, COLS, C), BF16),
            V((3 * FS, ROWS, COLS, C), BF16),
            V((FS, ROWS, COLS, 3 * C), BF16),
            V((C, FS * ROWS * COLS), BF16),
            V((ROWS + 2, FS, COLS, 3 * C), BF16),
            V((3, 3 * C, C), BF16),
            V((3, 3 * C, C), BF16),
            V((3 * C, C), BF16),
            V((3 * C, C), BF16),
            V((2, 2 * FS, C), F32),
            V((2, NZ - 1, 2 * FS, C), F32),
            V((4, FS, C), F32),
            V((4, C, 3 * C), F32),
            V((4, C // 2, 3 * C), BF16),
            V((4, C // 2, 3 * C), BF16),
            V((4, C // 2, 3 * C), F32),
            V((4, C // 2, 3 * C), BF16),
            V((4, 3, 32, 3 * C), BF16),
            V((4, 4, 16, 384), F32),
            V((4, 4, 16, 384), BF16),
            V((4, 3, 16, 384), BF16),
            V((NZ, 8, 384), F32),
            V((NZ - 1, 8, 384), F32),
            V((NZ, 8, 384), F32),
            V((4, 2, 4, 4, 16, 384), BF16),
            V((2,) + shape, BF16),
            DMA((13,)),
            DMA((8,)),
            DMA((8,)),
            DMA((28,)),
            DMA((28,)),
            DMA((4, 14)),
            DMA((4, 14)),
        ],
        compiler_params=pltpu.CompilerParams(
            collective_id=0, has_side_effects=True, vmem_limit_bytes=58 * 1024 * 1024
        ),
        cost_estimate=pl.CostEstimate(flops=9_700_000_000, bytes_accessed=9_000_000, transcendentals=0),
    )(
        frames_in,
        cotangent,
        spatial.reshape(3, 3 * C, C),
        temporal.reshape(3 * C, C),
        norm_gain.reshape(1, C),
        norm_shift.reshape(1, C),
        clip_frames,
        dilation,
    )
    out_frames = (frames_in.astype(F32) + tout.astype(F32)).astype(BF16)
    grads = ag.reshape(4, 8, 2, 2, 16, 384).transpose(0, 1, 2, 4, 3, 5).reshape(4, C, 3, C)
    grads = grads.transpose(0, 2, 1, 3).astype(F32)
    return out_frames, ig, grads[1:], grads[0]


def solution(mesh):
    frames = P("tm", "space", None, None)
    return jax.shard_map(
        section,
        mesh=mesh,
        in_specs=(frames, frames, P(), P(), P(), P(), P(), P()),
        out_specs=(frames, frames, P(), P()),
        check_vma=False,
    )
```

time: 477 us -> 96 us (0.20)
  waiting for transfers between devices: 254 us -> 0 us
  Pallas kernels: 0 us -> 79.1 us
  matrix products: 65.7 us -> 0 us
  starting transfers between devices: 49.8 us -> 0 us
  blocking collectives: 29.4 us -> 0 us
  other arithmetic: 31.4 us -> 2.73 us
  between operations: 20 us -> 0.69 us
  local copies, waits for them, and re-layouts: 24.2 us -> 13.3 us
    psum x1 -> x0, waiting for transfers between devices: 248 us -> none  [per_device(): lax.psum((spatial_part, temporal_part), ('tm', 'space'))]
    pallas_call x0 -> x1, Pallas kernels: none -> 79.1 us  [section(): pl.pallas_call(kernel, out_shape=(jax.ShapeDtypeStruct(shape, BF16), jax....]
    dot_general x36 -> x0, matrix products: 65.7 us -> none  [the longest x9 23.7 us: spatial_forward(): jnp.dot(window, spatial[offset_row, offset_col], preferred_element_type=j...]
    all_to_all x4 -> x0, starting transfers between devices: 38 us -> none  [the longest x1 15.1 us: per_device(): lax.all_to_all(activation, 'tm', split_axis=1, concat_axis=0, tiled=True)]
    psum x2 -> x0, blocking collectives: 29.4 us -> none  [the longest x1 17.5 us: per_device(): lax.psum((group_fold(jnp.sum(conv_out, axis=(1, 2))), group_fold(jnp.sum(...]
    ppermute x4 -> x0, starting transfers between devices: 11.8 us -> none  [the longest x2 9.08 us: extended(): before = lax.ppermute(last, axis, up)]
    select_n x4 -> x0, other arithmetic: 10.3 us -> none  [shifted_pieces(): combined = jnp.where(keep_mask[:, None, None], shifted, combined)]
    unnamed x60 -> x9, local copies, waits for them, and re-layouts: 11.2 us -> 3.82 us
  transfers between devices with their start and end apart: 9 -> 0, of which waited for: 2 -> 0; matrix products, arithmetic and copies ran while one was open for 14% -> 0% of each run, Pallas kernels for 0% -> 0%
where the time goes in v1:
time: 96 us; the launch traced here: 95.8 us
  Pallas kernels  79.1 us (82%)
  local copies, waits for them, and re-layouts  13.3 us (14%)
  other arithmetic  2.73 us (3%)
    pallas_call x1, Pallas kernels, section(): pl.pallas_call(kernel, out_shape=(jax.ShapeDtypeStruct(shape, BF16), jax....  79.1 us
    convert_element_type x2, local copies, waits for them, and re-layouts, section(): grads = grads.transpose(0, 2, 1, 3).astype(F32)  5.67 us
    unnamed x9, local copies, waits for them, and re-layouts  3.82 us
    convert_element_type x1, other arithmetic, section(): out_frames = (frames_in.astype(F32) + tout.astype(F32)).astype(BF16)  2.73 us
    slice x1, local copies, waits for them, and re-layouts, section(): return (out_frames, ig, grads[1:], grads[0])  2.43 us

profile of v1, /device:TPU:1, one launch (start us, length us, event | category | flops | bytes accessed | tf_op | source)
XLA Modules:
  0.0 95.8 jit_solution(14718927643206217844)
XLA Ops:
  0.6 0.0 copy-start.1
  0.6 79.1 %shard_map.111 = (bf16[8,4,64,256]{3,2,1,0:T(8,128)(2,1)}, bf16[8,4,64,256]{3,2,1,0:T(8,128)(2,1)}, bf16[4,2,4,4,16,384]{5,4,3,2,1,0:T(8,128)(2,1)}) custom-call(bf16[8,4,64,256]{3,2,1,0:T(8,128)(2,1)} %fr.1, bf16[8,4,64,256]{3,2,1,0:T(8,128)(2,1)} %ct.1, bf16[3,768,256]{2,1,0:T(8,128)(2,1)} %bitcast.16, bf16[768,256]{1,0:T(8,128)(2,1)} %bitcast.17, ...), custom_call_target="tpu_custom_call" | custom-call | flops 9699999744 | bytes 9000000 | tf_op jit(solution)/shard_map/pallas_call | solution.py:455
  79.8 0.0 copy-start
  79.8 0.0 copy-done.1
  79.8 2.7 %add_convert_fusion = bf16[8,4,64,256]{3,2,1,0:T(8,128)(2,1)} fusion(bf16[8,4,64,256]{3,2,1,0:T(8,128)(2,1)} %get-tuple-element.7, bf16[8,4,64,256]{3,2,1,0:T(8,128)(2,1)S(1)} %copy-done.1), kind=kLoop, calls=%fused_computation.1 | loop fusion | flops 2097152 | bytes 3145728 | tf_op jit(solution)/shard_map/convert_element_type | solution.py:518
  82.5 0.0 copy-done
  82.5 1.2 %copy.16 = f32[4,8,2,2,16,384]{5,3,4,2,1,0:T(2,128)S(1)} copy(bf16[4,8,2,2,16,384]{5,4,3,2,1,0:T(8,128)(2,1)S(1)} %bitcast.15) | data formatting | bytes 4718592 | tf_op jit(solution)/shard_map/convert_element_type | solution.py:520
  83.7 4.5 %reshape.30 = f32[4,256,3,256]{3,2,1,0:T(4,128)} reshape(f32[4,8,2,16,2,384]{5,4,3,2,1,0:T(2,128)S(1)} %bitcast.14) | data formatting | bytes 6291456 | tf_op jit(solution)/shard_map/convert_element_type | solution.py:520
  88.2 1.4 %slice_bitcast_fusion = f32[3,256,256]{2,0,1:T(4,128)S(1)} fusion(f32[4,3,256,256]{3,1,2,0:T(4,128)} %bitcast.12), kind=kLoop, calls=%fused_computation.2 | loop fusion | bytes 1572864 | tf_op jit(solution)/shard_map/squeeze | solution.py:521
  89.6 2.4 %slice.8 = f32[3,3,256,256]{3,1,2,0:T(4,128)S(1)} slice(f32[4,3,256,256]{3,1,2,0:T(4,128)} %bitcast.13), slice={[1:4], [0:3], [0:256], [0:256]} | slice | bytes 4718592 | tf_op jit(solution)/shard_map/slice | solution.py:521
  92.0 0.0 copy-start.2
  92.0 1.8 %copy.13 = f32[3,3,256,256]{3,2,1,0:T(8,128)} copy(f32[3,3,256,256]{3,1,2,0:T(4,128)S(1)} %slice.8) | data formatting | bytes 4718592
  93.8 1.0 %copy.14 = f32[3,256,256]{2,1,0:T(8,128)} copy(f32[3,256,256]{2,0,1:T(4,128)S(1)} %slice_bitcast_fusion) | data formatting | bytes 1572864
  94.9 0.0 copy-done.2
  94.9 1.0 %copy.18 = bf16[8,4,64,256]{3,2,1,0:T(8,128)(2,1)} copy(bf16[8,4,64,256]{3,2,1,0:T(8,128)(2,1)S(1)} %copy-done.2) | data formatting | bytes 2097152
Async XLA Ops:
  0.6 79.1 %copy-start.1 = (bf16[8,4,64,256]{3,2,1,0:T(8,128)(2,1)S(1)}, bf16[8,4,64,256]{3,2,1,0:T(8,128)(2,1)}, u32[]{:S(2)}) copy-start(bf16[8,4,64,256]{3,2,1,0:T(8,128)(2,1)} %fr.1) | copy-start | bytes 3145732
  79.8 2.8 %copy-start = (bf16[4,2,4,4,16,384]{5,4,3,2,1,0:T(8,128)(2,1)S(1)}, bf16[4,2,4,4,16,384]{5,4,3,2,1,0:T(8,128)(2,1)}, u32[]{:S(2)}) copy-start(bf16[4,2,4,4,16,384]{5,4,3,2,1,0:T(8,128)(2,1)} %get-tuple-element.9) | copy-start | bytes 4718596
  92.0 2.8 %copy-start.2 = (bf16[8,4,64,256]{3,2,1,0:T(8,128)(2,1)S(1)}, bf16[8,4,64,256]{3,2,1,0:T(8,128)(2,1)}, u32[]{:S(2)}) copy-start(bf16[8,4,64,256]{3,2,1,0:T(8,128)(2,1)} %get-tuple-element.19) | copy-start | bytes 3145732

commit v2 on v1

--- a/solution.py
+++ b/solution.py
@@ -50,7 +50,7 @@
     tout, ig_out, ag_out,
     xs3, xt, convf, dh, gn, a24, c24, pieces, at, gs3, w3, wt3, t3, tt3,
     st_loc, st_recv, st_fin, wg, s1h, r1, s1, s1c, r2, s2, s2c, r3, zf, zrecv, zag, agb, outv,
-    lsem, bsend, brecv, ssend, srecv, rsend, rrecv,
+    lsem, osem, bsend, brecv, ssend, srecv, rsend, rrecv,
 ):
     tm = lax.axis_index("tm")
     sp = lax.axis_index("space")
@@ -142,6 +142,22 @@
     loads[4].wait()
     loop(1, ROWS - 1, conv_row)
 
+    def edge_start(t):
+        line = 1 + t * (ROWS - 2)
+        acc = dot(xs3[line].reshape(LINE, 3 * C), w3[1 - t])
+        acc = acc + dot(xs3[line + 1].reshape(LINE, 3 * C), w3[2 - t])
+        convf[t * (ROWS - 1)] = acc.reshape(FS, COLS, C)
+
+    def edge_finish(t):
+        r = t * (ROWS - 1)
+        acc = dot(xs3[t * (ROWS + 1)].reshape(LINE, 3 * C), w3[2 * t])
+        acc = acc.reshape(FS, COLS, C) + convf[r]
+        convf[r] = acc
+        st_loc[0, pl.ds(0, FS)] += jnp.sum(acc, axis=1)
+        st_loc[0, pl.ds(FS, FS)] += jnp.sum(acc * acc, axis=1)
+
+    loop(0, 2, edge_start)
+
     def transpose_line(line):
         x = xs3[line, :, :, MID].reshape(LINE, C)
         xt[:, pl.ds(pl.multiple_of(line * LINE, LINE), LINE)] = x.T
@@ -163,7 +179,7 @@
     widen_row(xs3, 0, 1, not_first)
     halo_x[1].wait_recv()
     widen_row(xs3, ROWS + 1, 1, not_last)
-    loop(0, 2, lambda t: conv_row(t * (ROWS - 1)))
+    loop(0, 2, edge_finish)
 
     def exchange_stats(phase):
         copies = []
@@ -218,25 +234,26 @@
     ]
     sends += halo_a
 
-    def gather(source, f, direction):
+    def gather(source, f, direction, taps):
         frame = tm * FS + f
         second = (frame >= first).astype(jnp.int32)
         gap = jnp.where(second == 1, dl[1], dl[0])
-        for k in range(3):
+        for k in taps:
             move = direction * (k - 1) * gap
             target = frame + move
             same = (target >= first).astype(jnp.int32) == second
             live = (frame < filled) & (target >= 0) & (target < filled) & same
             slot = jnp.clip(FS + f + move, 0, 3 * FS - 1)
-            v = source[slot].astype(F32) * live.astype(F32)
-            pieces[f, :, :, pl.ds(k * C, C)] = v.astype(BF16)
+            keep = jnp.full((ROWS, COLS, C), live.astype(F32)).astype(BF16)
+            pieces[f, :, :, pl.ds(k * C, C)] = source[slot] * keep
 
     loads[6].wait()
+    loop(0, FS, lambda f: gather(c24, f, -1, (1,)))
     for copy in halo_c:
         copy.wait_recv()
 
     def backward_time(f):
-        gather(c24, f, -1)
+        gather(c24, f, -1, (0, 2))
         back = dot(pieces[f].reshape(ROWS * COLS, 3 * C), tt3[...]).astype(BF16).astype(F32)
         grad = back * dh[:, f].reshape(ROWS * COLS, C)
         gn[:, f] = grad.reshape(ROWS, COLS, C)
@@ -248,8 +265,8 @@
     stats = exchange_stats(1)
     sends += stats
 
-    first_axis = [(at_y, yi), (at_x, xi), (at_y, yi), (at_x, xi)]
-    second_axis = [(at_x, xi), (at_y, yi), (at_x, xi), (at_y, yi)]
+    first_axis = [(at_y, yi), (at_x, xi), (at_x, xi), (at_y, yi)]
+    second_axis = [(at_x, xi), (at_y, yi), (at_y, yi), (at_x, xi)]
     half = C // 2
     stage1 = [None] * 4
     stage2 = [None] * 4
@@ -350,9 +367,10 @@
             xt[:, pl.ds(i * LINE, ROWS * LINE)], gs3[pl.ds(1, ROWS)].reshape(ROWS * LINE, 3 * C)
         )
         begin1(i + 1)
+        if i > 0:
+            begin2(i)
+    begin2(3)
     begin3(0)
-    for b in (1, 2, 3):
-        begin2(b)
 
     def in_row(r):
         acc = dot(gs3[r + 2].reshape(LINE, 3 * C), wt3[0])
@@ -394,10 +412,10 @@
         copy.wait_recv()
 
     def forward_time(f):
-        gather(a24, f, 1)
-        outv[1, f] = (
-            dot(pieces[f].reshape(ROWS * COLS, 3 * C), t3[...]).astype(BF16).reshape(ROWS, COLS, C)
-        )
+        gather(a24, f, 1, (0, 1, 2))
+        moved = dot(pieces[f].reshape(ROWS * COLS, 3 * C), t3[...]).astype(BF16).astype(F32)
+        x = xs3[pl.ds(1, ROWS), f, :, MID].astype(F32)
+        outv[1, f] = (x + moved.reshape(ROWS, COLS, C)).astype(BF16)
 
     loop(0, FS, forward_time)
     out_t = pltpu.make_async_copy(outv.at[1], tout, lsem.at[8])
@@ -426,22 +444,73 @@
         )
         sends += g2[b]
     g1 = []
-    for b in range(4):
-        for copy in g2[b]:
-            copy.wait_recv()
-        here = agb.at[b, core]
-        g1.append(remote(here, here, rsend.at[b, 13], rrecv.at[b, 13], (pair, sp)))
-    sends += g1
     out_g = []
     for b in range(4):
-        g1[b].wait_recv()
-        out_g.append(pltpu.make_async_copy(agb.at[b], ag_out.at[b], lsem.at[9 + b]))
-        out_g[b].start()
+        n1 = first_axis[b][1]
+        for o in range(4):
+            if o > 0:
+                g2[b][o - 1].wait_recv()
+            here = lax.rem(n1 + 4 - o, 4)
+            g1.append(
+                remote(
+                    agb.at[b, core, here], ag_out.at[b, core, here], rsend.at[b, 13 + o],
+                    rrecv.at[b, 13 + o], (pair, sp),
+                )
+            )
+            out_g.append(
+                pltpu.make_async_copy(agb.at[b, core, here], ag_out.at[b, core, here], osem.at[b, o])
+            )
+            out_g[-1].start()
+    sends += g1
+    for copy in g1:
+        copy.wait_recv()
     for copy in sends:
         copy.wait_send()
     out_ig.wait()
     out_t.wait()
     for copy in out_g:
+        copy.wait()
+
+
+def deliver(of_in, ig_in, ag, of, ig, sg, tg, agv, full, frames, csem, gsem):
+    loads = [pltpu.make_async_copy(ag.at[b], agv.at[b], gsem.at[b]) for b in range(4)]
+    for load in loads:
+        load.start()
+    quarter = FS // 4
+    parts = []
+    for n in range(4):
+        part = pl.ds(n * quarter, quarter)
+        parts.append((of_in.at[part], frames.at[0, part], of.at[part], csem.at[0, n]))
+        parts.append((ig_in.at[part], frames.at[1, part], ig.at[part], csem.at[1, n]))
+    arrivals = [pltpu.make_async_copy(source, stage, sem) for source, stage, _, sem in parts]
+    for copy in arrivals:
+        copy.start()
+    copies = []
+    for copy, (_, stage, target, sem) in zip(arrivals, parts):
+        copy.wait()
+        copies.append(pltpu.make_async_copy(stage, target, sem))
+        copies[-1].start()
+    stores = []
+    for b in range(4):
+        loads[b].wait()
+
+        def place(m, carry):
+            for q in range(4):
+                rows = pl.ds(pl.multiple_of(m * 32 + (q // 2) * 16, 16), 16)
+                v = agv[b, lax.div(m, 4), lax.rem(m, 4), q].astype(F32)
+                if q % 2 == 0:
+                    full[3 * b, rows, :] = v[:, 0:C]
+                    full[3 * b + 1, rows, pl.ds(0, 128)] = v[:, C:384]
+                else:
+                    full[3 * b + 1, rows, pl.ds(128, 128)] = v[:, 0:128]
+                    full[3 * b + 2, rows, :] = v[:, 128:384]
+            return carry
+
+        lax.fori_loop(0, 8, place, 0)
+        target = tg if b == 0 else sg.at[pl.ds(3 * (b - 1), 3)]
+        stores.append(pltpu.make_async_copy(full.at[pl.ds(3 * b, 3)], target, gsem.at[b]))
+        stores[b].start()
+    for copy in copies + stores:
         copy.wait()
 
 
@@ -493,13 +562,14 @@
             V((NZ, 8, 384), F32),
             V((4, 2, 4, 4, 16, 384), BF16),
             V((2,) + shape, BF16),
-            DMA((13,)),
+            DMA((9,)),
+            DMA((4, 4)),
             DMA((8,)),
             DMA((8,)),
             DMA((28,)),
             DMA((28,)),
-            DMA((4, 14)),
-            DMA((4, 14)),
+            DMA((4, 17)),
+            DMA((4, 17)),
         ],
         compiler_params=pltpu.CompilerParams(
             collective_id=0, has_side_effects=True, vmem_limit_bytes=58 * 1024 * 1024
@@ -515,10 +585,21 @@
         clip_frames,
         dilation,
     )
-    out_frames = (frames_in.astype(F32) + tout.astype(F32)).astype(BF16)
-    grads = ag.reshape(4, 8, 2, 2, 16, 384).transpose(0, 1, 2, 4, 3, 5).reshape(4, C, 3, C)
-    grads = grads.transpose(0, 2, 1, 3).astype(F32)
-    return out_frames, ig, grads[1:], grads[0]
+    out_frames, in_grad, spatial_grad, temporal_grad = pl.pallas_call(
+        deliver,
+        out_shape=(
+            jax.ShapeDtypeStruct(shape, BF16),
+            jax.ShapeDtypeStruct(shape, BF16),
+            jax.ShapeDtypeStruct((9, C, C), F32),
+            jax.ShapeDtypeStruct((3, C, C), F32),
+        ),
+        in_specs=[any_spec] * 3,
+        out_specs=(any_spec,) * 4,
+        scratch_shapes=[V((4, 2, 4, 4, 16, 384), BF16), V((12, C, C), F32), V((2,) + shape, BF16), DMA((2, 4)), DMA((4,))],
+        compiler_params=pltpu.CompilerParams(vmem_limit_bytes=58 * 1024 * 1024),
+        cost_estimate=pl.CostEstimate(flops=0, bytes_accessed=9_000_000, transcendentals=0),
+    )(tout, ig, ag)
+    return out_frames, in_grad, spatial_grad.reshape(3, 3, C, C), temporal_grad
 
 
 def solution(mesh):

time: 96 us -> 79.3 us (0.83)
  local copies, waits for them, and re-layouts: 13.3 us -> 0 us
  other arithmetic: 2.73 us -> 0 us
    convert_element_type x2 -> x0, local copies, waits for them, and re-layouts: 5.67 us -> none  [section(): grads = grads.transpose(0, 2, 1, 3).astype(F32)]
    pallas_call x1, Pallas kernels: 79.1 us -> 74.3 us  [section(): pl.pallas_call(kernel, out_shape=(jax.ShapeDtypeStruct(shape, BF16), jax....]
    pallas_call x0 -> x1, Pallas kernels: none -> 4.18 us  [section(): pl.pallas_call(deliver, out_shape=(jax.ShapeDtypeStruct(shape, BF16), jax...]
    unnamed x9 -> x0, local copies, waits for them, and re-layouts: 3.82 us -> none
    convert_element_type x1 -> x0, other arithmetic: 2.73 us -> none  [section(): out_frames = (frames_in.astype(F32) + tout.astype(F32)).astype(BF16)]
    slice x1 -> x0, local copies, waits for them, and re-layouts: 2.43 us -> none  [section(): return (out_frames, ig, grads[1:], grads[0])]
    squeeze x1 -> x0, local copies, waits for them, and re-layouts: 1.4 us -> none  [section(): return (out_frames, ig, grads[1:], grads[0])]
where the time goes in v2:
time: 79.3 us; the launch traced here: 79.2 us
  Pallas kernels  78.5 us (99%)
    pallas_call x1, Pallas kernels, section(): pl.pallas_call(kernel, out_shape=(jax.ShapeDtypeStruct(shape, BF16), jax....  74.3 us
    pallas_call x1, Pallas kernels, section(): pl.pallas_call(deliver, out_shape=(jax.ShapeDtypeStruct(shape, BF16), jax...  4.18 us

profile of v2, /device:TPU:1, one launch (start us, length us, event | category | flops | bytes accessed | tf_op | source)
XLA Modules:
  0.0 79.2 jit_solution(7112249089228179033)
XLA Ops:
  0.6 74.3 %shard_map.111 = (bf16[8,4,64,256]{3,2,1,0:T(8,128)(2,1)}, bf16[8,4,64,256]{3,2,1,0:T(8,128)(2,1)}, bf16[4,2,4,4,16,384]{5,4,3,2,1,0:T(8,128)(2,1)}) custom-call(bf16[8,4,64,256]{3,2,1,0:T(8,128)(2,1)} %fr.1, bf16[8,4,64,256]{3,2,1,0:T(8,128)(2,1)} %ct.1, bf16[3,768,256]{2,1,0:T(8,128)(2,1)} %bitcast.6, bf16[768,256]{1,0:T(8,128)(2,1)} %bitcast.7, ...), custom_call_target="tpu_custom_call" | custom-call | flops 9699999744 | bytes 9000000 | tf_op jit(solution)/shard_map/pallas_call | solution.py:524
  75.0 4.2 %shard_map.112 = (bf16[8,4,64,256]{3,2,1,0:T(8,128)(2,1)}, bf16[8,4,64,256]{3,2,1,0:T(8,128)(2,1)}, f32[9,256,256]{2,1,0:T(8,128)}, f32[3,256,256]{2,1,0:T(8,128)}) custom-call(bf16[8,4,64,256]{3,2,1,0:T(8,128)(2,1)} %get-tuple-element.11.of_in, bf16[8,4,64,256]{3,2,1,0:T(8,128)(2,1)} %get-tuple-element.12.ig_in, ...), custom_call_target="tpu_custom_call" | custom-call | bytes 9000000 | tf_op jit(solution)/shard_map/pallas_call | solution.py:588

commit v3 on v2

--- a/solution.py
+++ b/solution.py
@@ -22,6 +22,7 @@
 ENTRIES = float(ROWS * NZ * COLS * 8)
 EPS = 1e-05
 MID = pl.ds(C, C)
+FAR_FIRST = (4, 3, 5, 2, 6, 1, 7)
 
 
 def dot(a, b):
@@ -46,10 +47,11 @@
 
 
 def kernel(
-    fr, ct, w_in, t_in, gain_ref, shift_ref, cf, dl,
+    fr, ct, w_in, t_in, gain_in, shift_in, cf_in, dl_in,
     tout, ig_out, ag_out,
     xs3, xt, convf, dh, gn, a24, c24, pieces, at, gs3, w3, wt3, t3, tt3,
     st_loc, st_recv, st_fin, wg, s1h, r1, s1, s1c, r2, s2, s2c, r3, zf, zrecv, zag, agb, outv,
+    gain_ref, shift_ref, cf, dl,
     lsem, osem, bsend, brecv, ssend, srecv, rsend, rrecv,
 ):
     tm = lax.axis_index("tm")
@@ -76,15 +78,6 @@
         copy.start()
         return copy
 
-    loads = [
-        pltpu.make_async_copy(fr.at[:, r], xs3.at[r + 1, :, :, MID], lsem.at[r]) for r in range(ROWS)
-    ]
-    loads.append(pltpu.make_async_copy(w_in, w3, lsem.at[4]))
-    loads.append(pltpu.make_async_copy(t_in, t3, lsem.at[5]))
-    loads.append(pltpu.make_async_copy(ct, c24.at[pl.ds(FS, FS)], lsem.at[6]))
-    for load in loads:
-        load.start()
-
     far = tm + (2 * core - 1)
     far = lax.rem(far + NTM, NTM)
     partners = [(pair, sp), (far, sp)]
@@ -94,6 +87,17 @@
     barrier = pltpu.get_barrier_semaphore()
     for partner in partners:
         pl.semaphore_signal(barrier, inc=1, device_id=partner, device_id_type=MESH)
+    loads = [
+        pltpu.make_async_copy(fr.at[:, r], xs3.at[r + 1, :, :, MID], lsem.at[r]) for r in range(ROWS)
+    ]
+    loads.append(pltpu.make_async_copy(w_in, w3, lsem.at[4]))
+    loads.append(pltpu.make_async_copy(t_in, t3, lsem.at[5]))
+    loads.append(pltpu.make_async_copy(ct, c24.at[pl.ds(FS, FS)], lsem.at[6]))
+    small = [(gain_in, gain_ref), (shift_in, shift_ref), (cf_in, cf), (dl_in, dl)]
+    loads += [pltpu.make_async_copy(source, target, lsem.at[9 + n]) for n, (source, target) in enumerate(small)]
+    for load in loads:
+        load.start()
+
     pl.semaphore_wait(barrier, len(partners))
 
     sends = []
@@ -182,26 +186,24 @@
     loop(0, 2, edge_finish)
 
     def exchange_stats(phase):
-        copies = []
-        for o in range(1, NZ):
+        copies = {}
+        for o in FAR_FIRST:
             n = phase * (NZ - 1) + o - 1
-            copies.append(
-                remote(
-                    st_loc.at[phase], st_recv.at[phase, o - 1], ssend.at[n], srecv.at[n],
-                    (tm, lax.rem(sp + o, NZ)),
-                )
+            copies[o] = remote(
+                st_loc.at[phase], st_recv.at[phase, o - 1], ssend.at[n], srecv.at[n],
+                (tm, lax.rem(sp + o, NZ)),
             )
+        sends.extend(copies.values())
         return copies
 
     def total_stats(phase, copies):
         total = st_loc[phase]
         for o in range(1, NZ):
-            copies[o - 1].wait_recv()
+            copies[o].wait_recv()
             total = total + st_recv[phase, o - 1]
         return fold8(total) * (1.0 / ENTRIES)
 
     stats = exchange_stats(0)
-    sends += stats
     loop(0, 2, lambda t: transpose_line(t * (ROWS + 1)))
     total = total_stats(0, stats)
     mean = total[0:FS]
@@ -209,6 +211,8 @@
     st_fin[0] = mean
     st_fin[1] = lax.rsqrt(variance + EPS)
 
+    for load in loads[7:]:
+        load.wait()
     first = cf[0]
     filled = cf[0] + cf[1]
     gain = gain_ref[...]
@@ -263,7 +267,6 @@
 
     loop(0, FS, backward_time)
     stats = exchange_stats(1)
-    sends += stats
 
     first_axis = [(at_y, yi), (at_x, xi), (at_x, xi), (at_y, yi)]
     second_axis = [(at_x, xi), (at_y, yi), (at_y, yi), (at_x, xi)]
@@ -388,22 +391,22 @@
     widen_row(gs3, ROWS + 1, -1, not_last)
     for b in range(4):
         finish3(b)
-    z1 = []
-    for o in range(1, NZ):
+    z1 = {}
+    for o in FAR_FIRST:
         q = lax.rem(sp + o, NZ)
-        z1.append(remote(zf.at[q], zrecv.at[o - 1], ssend.at[13 + o], srecv.at[13 + o], (tm, q)))
-    sends += z1
+        z1[o] = (remote(zf.at[q], zrecv.at[o - 1], ssend.at[13 + o], srecv.at[13 + o], (tm, q)))
+    sends += z1.values()
     loop(0, 2, lambda t: in_row(t * (ROWS - 1)))
     out_ig = pltpu.make_async_copy(outv.at[0], ig_out, lsem.at[7])
     out_ig.start()
 
     v = zf[sp]
     for o in range(1, NZ):
-        z1[o - 1].wait_recv()
+        z1[o].wait_recv()
         v = v + zrecv[o - 1]
     zag[sp] = v
     z2 = []
-    for o in range(1, NZ):
+    for o in FAR_FIRST:
         q = lax.rem(sp + o, NZ)
         z2.append(remote(zag.at[sp], zag.at[sp], ssend.at[20 + o], srecv.at[20 + o], (tm, q)))
     sends += z2
@@ -430,31 +433,32 @@
         place = second_axis[b][0]
         here = agb.at[b, core, n1, n2]
         g3.append(
-            [remote(here, here, rsend.at[b, 6 + o], rrecv.at[b, 6 + o], (place(o), sp)) for o in range(1, 4)]
+            [remote(here, here, rsend.at[b, 6 + o], rrecv.at[b, 6 + o], (place(o), sp)) for o in (2, 1, 3)]
         )
         sends += g3[b]
-    g2 = []
-    for b in range(4):
-        for copy in g3[b]:
-            copy.wait_recv()
-        place, n1 = first_axis[b]
-        here = agb.at[b, core, n1]
-        g2.append(
-            [remote(here, here, rsend.at[b, 9 + o], rrecv.at[b, 9 + o], (place(o), sp)) for o in range(1, 4)]
-        )
-        sends += g2[b]
+    g2 = [{} for _ in range(4)]
+    for c in (0, 1, 3, 2):
+        for b in range(4):
+            if c > 0:
+                g3[b][(2, 1, 3).index(c)].wait_recv()
+            place, n1 = first_axis[b]
+            here = agb.at[b, core, n1, lax.rem(second_axis[b][1] + 4 - c, 4)]
+            for o in (2, 1, 3):
+                n = 6 + 4 * o + c
+                g2[b][o, c] = remote(here, here, rsend.at[b, n], rrecv.at[b, n], (place(o), sp))
+            sends += [g2[b][o, c] for o in (2, 1, 3)]
     g1 = []
     out_g = []
-    for b in range(4):
-        n1 = first_axis[b][1]
-        for o in range(4):
+    for o in (0, 1, 3, 2):
+        for b in range(4):
             if o > 0:
-                g2[b][o - 1].wait_recv()
-            here = lax.rem(n1 + 4 - o, 4)
+                for c in (0, 1, 3, 2):
+                    g2[b][o, c].wait_recv()
+            here = lax.rem(first_axis[b][1] + 4 - o, 4)
             g1.append(
                 remote(
-                    agb.at[b, core, here], ag_out.at[b, core, here], rsend.at[b, 13 + o],
-                    rrecv.at[b, 13 + o], (pair, sp),
+                    agb.at[b, core, here], ag_out.at[b, core, here], rsend.at[b, 22 + o],
+                    rrecv.at[b, 22 + o], (pair, sp),
                 )
             )
             out_g.append(
@@ -485,11 +489,6 @@
     arrivals = [pltpu.make_async_copy(source, stage, sem) for source, stage, _, sem in parts]
     for copy in arrivals:
         copy.start()
-    copies = []
-    for copy, (_, stage, target, sem) in zip(arrivals, parts):
-        copy.wait()
-        copies.append(pltpu.make_async_copy(stage, target, sem))
-        copies[-1].start()
     stores = []
     for b in range(4):
         loads[b].wait()
@@ -510,14 +509,17 @@
         target = tg if b == 0 else sg.at[pl.ds(3 * (b - 1), 3)]
         stores.append(pltpu.make_async_copy(full.at[pl.ds(3 * b, 3)], target, gsem.at[b]))
         stores[b].start()
+    copies = []
+    for copy, (_, stage, target, sem) in zip(arrivals, parts):
+        copy.wait()
+        copies.append(pltpu.make_async_copy(stage, target, sem))
+        copies[-1].start()
     for copy in copies + stores:
         copy.wait()
 
 
 def section(frames_in, cotangent, spatial, temporal, norm_gain, norm_shift, clip_frames, dilation):
     any_spec = pl.BlockSpec(memory_space=pl.ANY)
-    vmem_spec = pl.BlockSpec(memory_space=pltpu.VMEM)
-    smem_spec = pl.BlockSpec(memory_space=pltpu.SMEM)
     shape = (FS, ROWS, COLS, C)
     V = pltpu.VMEM
     DMA = pltpu.SemaphoreType.DMA
@@ -528,7 +530,7 @@
             jax.ShapeDtypeStruct(shape, BF16),
             jax.ShapeDtypeStruct((4, 2, 4, 4, 16, 384), BF16),
         ),
-        in_specs=[any_spec] * 4 + [vmem_spec] * 2 + [smem_spec] * 2,
+        in_specs=[any_spec] * 8,
         out_specs=(any_spec, any_spec, any_spec),
         scratch_shapes=[
             V((ROWS + 2, FS, COLS, 3 * C), BF16),
@@ -562,14 +564,18 @@
             V((NZ, 8, 384), F32),
             V((4, 2, 4, 4, 16, 384), BF16),
             V((2,) + shape, BF16),
-            DMA((9,)),
+            V((1, C), F32),
+            V((1, C), F32),
+            pltpu.SMEM((2,), jnp.int32),
+            pltpu.SMEM((2,), jnp.int32),
+            DMA((13,)),
             DMA((4, 4)),
             DMA((8,)),
             DMA((8,)),
             DMA((28,)),
             DMA((28,)),
-            DMA((4, 17)),
-            DMA((4, 17)),
+            DMA((4, 26)),
+            DMA((4, 26)),
         ],
         compiler_params=pltpu.CompilerParams(
             collective_id=0, has_side_effects=True, vmem_limit_bytes=58 * 1024 * 1024

time: 79.3 us -> 75.3 us (0.950)
  Pallas kernels: 78.5 us -> 74.6 us
    pallas_call x1, Pallas kernels: 74.3 us -> 70.7 us  [section(): pl.pallas_call(kernel, out_shape=(jax.ShapeDtypeStruct(shape, BF16), jax....]
where the time goes in v3:
time: 75.3 us; the launch traced here: 75.2 us
  Pallas kernels  74.6 us (99%)
    pallas_call x1, Pallas kernels, section(): pl.pallas_call(kernel, out_shape=(jax.ShapeDtypeStruct(shape, BF16), jax....  70.7 us
    pallas_call x1, Pallas kernels, section(): pl.pallas_call(deliver, out_shape=(jax.ShapeDtypeStruct(shape, BF16), jax...  3.84 us

profile of v3, /device:TPU:1, one launch (start us, length us, event | category | flops | bytes accessed | tf_op | source)
XLA Modules:
  0.0 75.2 jit_solution(16967369336926143299)
XLA Ops:
  0.6 70.7 %shard_map.111 = (bf16[8,4,64,256]{3,2,1,0:T(8,128)(2,1)}, bf16[8,4,64,256]{3,2,1,0:T(8,128)(2,1)}, bf16[4,2,4,4,16,384]{5,4,3,2,1,0:T(8,128)(2,1)}) custom-call(bf16[8,4,64,256]{3,2,1,0:T(8,128)(2,1)} %fr.1, bf16[8,4,64,256]{3,2,1,0:T(8,128)(2,1)} %ct.1, bf16[3,768,256]{2,1,0:T(8,128)(2,1)} %bitcast.6, bf16[768,256]{1,0:T(8,128)(2,1)} %bitcast.7, ...), custom_call_target="tpu_custom_call" | custom-call | flops 9699999744 | bytes 9000000 | tf_op jit(solution)/shard_map/pallas_call | solution.py:526
  71.4 3.8 %shard_map.112 = (bf16[8,4,64,256]{3,2,1,0:T(8,128)(2,1)}, bf16[8,4,64,256]{3,2,1,0:T(8,128)(2,1)}, f32[9,256,256]{2,1,0:T(8,128)}, f32[3,256,256]{2,1,0:T(8,128)}) custom-call(bf16[8,4,64,256]{3,2,1,0:T(8,128)(2,1)} %get-tuple-element.11.of_in, bf16[8,4,64,256]{3,2,1,0:T(8,128)(2,1)} %get-tuple-element.12.ig_in, ...), custom_call_target="tpu_custom_call" | custom-call | bytes 9000000 | tf_op jit(solution)/shard_map/pallas_call | solution.py:594

commit v4 on v3

--- a/solution.py
+++ b/solution.py
@@ -230,13 +230,22 @@
         convf[:, f] = normed.reshape(ROWS, COLS, C)
         dh[:, f] = (sig * (1.0 + shaped * (1.0 - sig)) * gain).reshape(ROWS, COLS, C)
 
-    loop(0, FS, activate)
-    own = pl.ds(FS, FS)
-    halo_a = [
-        remote(a24.at[own], a24.at[pl.ds(0, FS)], bsend.at[4], brecv.at[4], (tm_next, sp)),
-        remote(a24.at[own], a24.at[pl.ds(2 * FS, FS)], bsend.at[5], brecv.at[5], (tm_prev, sp)),
-    ]
-    sends += halo_a
+    def send_activations(part):
+        width = FS // 2
+        mine = a24.at[pl.ds(FS + part * width, width)]
+        later = a24.at[pl.ds(part * width, width)]
+        earlier = a24.at[pl.ds(2 * FS + part * width, width)]
+        n = 4 + 4 * part
+        copies = [
+            remote(mine, later, bsend.at[n], brecv.at[n], (tm_next, sp)),
+            remote(mine, earlier, bsend.at[n + 1], brecv.at[n + 1], (tm_prev, sp)),
+        ]
+        sends.extend(copies)
+        return copies
+
+    loop(0, FS // 2, activate)
+    halo_a = send_activations(0)
+    loop(FS // 2, FS, activate)
 
     def gather(source, f, direction, taps):
         frame = tm * FS + f
@@ -275,16 +284,17 @@
     stage2 = [None] * 4
     stage3 = [None] * 4
 
-    def begin1(b):
-        other = pl.ds(pl.multiple_of((1 - core) * half, half), half)
-        s1h[b] = wg[b, other, :].astype(BF16)
+    theirs = pl.ds(pl.multiple_of((1 - core) * half, half), half)
+    mine = pl.ds(pl.multiple_of(core * half, half), half)
+
+    def begin1(b, product):
+        s1h[b] = product(theirs).astype(BF16)
         stage1[b] = remote(s1h.at[b], r1.at[b], rsend.at[b, 0], rrecv.at[b, 0], (pair, sp))
         sends.append(stage1[b])
 
     def begin2(b):
         stage1[b].wait_recv()
-        mine = pl.ds(pl.multiple_of(core * half, half), half)
-        v = wg[b, mine, :] + r1[b].astype(F32)
+        v = wg[b] + r1[b].astype(F32)
         s1[b] = v
         s1c[b] = v.astype(BF16)
         place, index = first_axis[b]
@@ -331,8 +341,12 @@
         at[:, pl.ds(pl.multiple_of(f * ROWS * COLS, ROWS * COLS), ROWS * COLS)] = x.T
 
     loop(0, FS, transpose_act)
-    wg[0] = dot(at[...], pieces[...].reshape(FS * ROWS * COLS, 3 * C))
-    begin1(0)
+
+    def time_product(rows):
+        return dot(at[rows, :], pieces[...].reshape(FS * ROWS * COLS, 3 * C))
+
+    begin1(0, time_product)
+    wg[0] = time_product(mine)
 
     total = total_stats(1, stats)
     st_fin[2] = total[0:FS]
@@ -365,14 +379,16 @@
     loop(0, FS, conv_grad_inner)
     begin2(0)
 
+    def space_product(i, rows):
+        return dot(
+            xt[rows, pl.ds(i * LINE, ROWS * LINE)], gs3[pl.ds(1, ROWS)].reshape(ROWS * LINE, 3 * C)
+        )
+
     for i in range(3):
-        wg[i + 1] = dot(
-            xt[:, pl.ds(i * LINE, ROWS * LINE)], gs3[pl.ds(1, ROWS)].reshape(ROWS * LINE, 3 * C)
-        )
-        begin1(i + 1)
-        if i > 0:
-            begin2(i)
-    begin2(3)
+        begin1(i + 1, functools.partial(space_product, i))
+    for i in range(3):
+        wg[i + 1] = space_product(i, mine)
+        begin2(i + 1)
     begin3(0)
 
     def in_row(r):
@@ -396,6 +412,7 @@
         q = lax.rem(sp + o, NZ)
         z1[o] = (remote(zf.at[q], zrecv.at[o - 1], ssend.at[13 + o], srecv.at[13 + o], (tm, q)))
     sends += z1.values()
+    halo_a += send_activations(1)
     loop(0, 2, lambda t: in_row(t * (ROWS - 1)))
     out_ig = pltpu.make_async_copy(outv.at[0], ig_out, lsem.at[7])
     out_ig.start()
@@ -411,19 +428,14 @@
         z2.append(remote(zag.at[sp], zag.at[sp], ssend.at[20 + o], srecv.at[20 + o], (tm, q)))
     sends += z2
 
-    for copy in halo_a:
-        copy.wait_recv()
-
     def forward_time(f):
         gather(a24, f, 1, (0, 1, 2))
         moved = dot(pieces[f].reshape(ROWS * COLS, 3 * C), t3[...]).astype(BF16).astype(F32)
         x = xs3[pl.ds(1, ROWS), f, :, MID].astype(F32)
         outv[1, f] = (x + moved.reshape(ROWS, COLS, C)).astype(BF16)
 
-    loop(0, FS, forward_time)
-    out_t = pltpu.make_async_copy(outv.at[1], tout, lsem.at[8])
-    out_t.start()
-
+    early_sends = sends
+    sends = []
     for copy in z2:
         copy.wait_recv()
     g3 = []
@@ -447,6 +459,14 @@
                 n = 6 + 4 * o + c
                 g2[b][o, c] = remote(here, here, rsend.at[b, n], rrecv.at[b, n], (place(o), sp))
             sends += [g2[b][o, c] for o in (2, 1, 3)]
+        if c == 0:
+            for copy in early_sends:
+                copy.wait_send()
+            for copy in halo_a:
+                copy.wait_recv()
+            loop(0, FS, forward_time)
+            out_t = pltpu.make_async_copy(outv.at[1], tout, lsem.at[8])
+            out_t.start()
     g1 = []
     out_g = []
     for o in (0, 1, 3, 2):
@@ -465,11 +485,10 @@
                 pltpu.make_async_copy(agb.at[b, core, here], ag_out.at[b, core, here], osem.at[b, o])
             )
             out_g[-1].start()
-    sends += g1
-    for copy in g1:
-        copy.wait_recv()
     for copy in sends:
         copy.wait_send()
+    for copy in g1:
+        copy.wait()
     out_ig.wait()
     out_t.wait()
     for copy in out_g:
@@ -550,7 +569,7 @@
             V((2, 2 * FS, C), F32),
             V((2, NZ - 1, 2 * FS, C), F32),
             V((4, FS, C), F32),
-            V((4, C, 3 * C), F32),
+            V((4, C // 2, 3 * C), F32),
             V((4, C // 2, 3 * C), BF16),
             V((4, C // 2, 3 * C), BF16),
             V((4, C // 2, 3 * C), F32),
@@ -570,8 +589,8 @@
             pltpu.SMEM((2,), jnp.int32),
             DMA((13,)),
             DMA((4, 4)),
-            DMA((8,)),
-            DMA((8,)),
+            DMA((10,)),
+            DMA((10,)),
             DMA((28,)),
             DMA((28,)),
             DMA((4, 26)),

time: 75.3 us -> 74.1 us (0.984)
  Pallas kernels: 74.6 us -> 73.4 us
    pallas_call x1, Pallas kernels: 70.7 us -> 69.5 us  [section(): pl.pallas_call(kernel, out_shape=(jax.ShapeDtypeStruct(shape, BF16), jax....]
where the time goes in v4:
time: 74.1 us; the launch traced here: 74 us
  Pallas kernels  73.4 us (99%)
    pallas_call x1, Pallas kernels, section(): pl.pallas_call(kernel, out_shape=(jax.ShapeDtypeStruct(shape, BF16), jax....  69.5 us
    pallas_call x1, Pallas kernels, section(): pl.pallas_call(deliver, out_shape=(jax.ShapeDtypeStruct(shape, BF16), jax...  3.84 us

profile of v4, /device:TPU:1, one launch (start us, length us, event | category | flops | bytes accessed | tf_op | source)
XLA Modules:
  0.0 74.0 jit_solution(16989366558967218255)
XLA Ops:
  0.6 69.5 %shard_map.111 = (bf16[8,4,64,256]{3,2,1,0:T(8,128)(2,1)}, bf16[8,4,64,256]{3,2,1,0:T(8,128)(2,1)}, bf16[4,2,4,4,16,384]{5,4,3,2,1,0:T(8,128)(2,1)}) custom-call(bf16[8,4,64,256]{3,2,1,0:T(8,128)(2,1)} %fr.1, bf16[8,4,64,256]{3,2,1,0:T(8,128)(2,1)} %ct.1, bf16[3,768,256]{2,1,0:T(8,128)(2,1)} %bitcast.6, bf16[768,256]{1,0:T(8,128)(2,1)} %bitcast.7, ...), custom_call_target="tpu_custom_call" | custom-call | flops 9699999744 | bytes 9000000 | tf_op jit(solution)/shard_map/pallas_call | solution.py:545
  70.2 3.8 %shard_map.112 = (bf16[8,4,64,256]{3,2,1,0:T(8,128)(2,1)}, bf16[8,4,64,256]{3,2,1,0:T(8,128)(2,1)}, f32[9,256,256]{2,1,0:T(8,128)}, f32[3,256,256]{2,1,0:T(8,128)}) custom-call(bf16[8,4,64,256]{3,2,1,0:T(8,128)(2,1)} %get-tuple-element.11.of_in, bf16[8,4,64,256]{3,2,1,0:T(8,128)(2,1)} %get-tuple-element.12.ig_in, ...), custom_call_target="tpu_custom_call" | custom-call | bytes 9000000 | tf_op jit(solution)/shard_map/pallas_call | solution.py:613

commit v5 on v4

--- a/solution.py
+++ b/solution.py
@@ -460,8 +460,6 @@
                 g2[b][o, c] = remote(here, here, rsend.at[b, n], rrecv.at[b, n], (place(o), sp))
             sends += [g2[b][o, c] for o in (2, 1, 3)]
         if c == 0:
-            for copy in early_sends:
-                copy.wait_send()
             for copy in halo_a:
                 copy.wait_recv()
             loop(0, FS, forward_time)
@@ -485,7 +483,7 @@
                 pltpu.make_async_copy(agb.at[b, core, here], ag_out.at[b, core, here], osem.at[b, o])
             )
             out_g[-1].start()
-    for copy in sends:
+    for copy in early_sends + sends:
         copy.wait_send()
     for copy in g1:
         copy.wait()

time: 74.1 us -> 74.1 us (level)
  no operation moved by 1% of the time
where the time goes in v5:
time: 74.1 us; the launch traced here: 74 us
  Pallas kernels  73.4 us (99%)
    pallas_call x1, Pallas kernels, section(): pl.pallas_call(kernel, out_shape=(jax.ShapeDtypeStruct(shape, BF16), jax....  69.5 us
    pallas_call x1, Pallas kernels, section(): pl.pallas_call(deliver, out_shape=(jax.ShapeDtypeStruct(shape, BF16), jax...  3.84 us

profile of v5, /device:TPU:1, one launch (start us, length us, event | category | flops | bytes accessed | tf_op | source)
XLA Modules:
  0.0 74.0 jit_solution(135565148215075616)
XLA Ops:
  0.6 69.5 %shard_map.111 = (bf16[8,4,64,256]{3,2,1,0:T(8,128)(2,1)}, bf16[8,4,64,256]{3,2,1,0:T(8,128)(2,1)}, bf16[4,2,4,4,16,384]{5,4,3,2,1,0:T(8,128)(2,1)}) custom-call(bf16[8,4,64,256]{3,2,1,0:T(8,128)(2,1)} %fr.1, bf16[8,4,64,256]{3,2,1,0:T(8,128)(2,1)} %ct.1, bf16[3,768,256]{2,1,0:T(8,128)(2,1)} %bitcast.6, bf16[768,256]{1,0:T(8,128)(2,1)} %bitcast.7, ...), custom_call_target="tpu_custom_call" | custom-call | flops 9699999744 | bytes 9000000 | tf_op jit(solution)/shard_map/pallas_call | solution.py:543
  70.2 3.8 %shard_map.112 = (bf16[8,4,64,256]{3,2,1,0:T(8,128)(2,1)}, bf16[8,4,64,256]{3,2,1,0:T(8,128)(2,1)}, f32[9,256,256]{2,1,0:T(8,128)}, f32[3,256,256]{2,1,0:T(8,128)}) custom-call(bf16[8,4,64,256]{3,2,1,0:T(8,128)(2,1)} %get-tuple-element.11.of_in, bf16[8,4,64,256]{3,2,1,0:T(8,128)(2,1)} %get-tuple-element.12.ig_in, ...), custom_call_target="tpu_custom_call" | custom-call | bytes 9000000 | tf_op jit(solution)/shard_map/pallas_call | solution.py:611
